TPU v7x, 32 devices: a whole 2x2x4 slice. The times are simulated.
32 devices in a mesh: space: 8 (over y, x, core), chan: 4 (over z).
Axes of the slice: x: 2, y: 2, z: 4, core: 2. Of those that a mesh axis runs over, the one named last changes fastest.
Arguments:
- positions: float32 [3, 4096], P(None, 'space'), may hold values from -6 to 6
- features: float32 [512, 4096], P('chan', 'space'), may hold values from -6 to 6
- block_counts: int32 [32], P('space'), may hold values from 64 to 128
- pair_table: int32 [3, 512], P(None, 'space'), may hold values from 0 to 31, as said below
- in_weight: float32 [2, 512, 512], P(None, 'chan'), may hold values from -0.25 to 0.25
- filter_weight: float32 [2, 8, 512], P(None, None, 'chan'), may hold values from -0.125 to 0.125
- mix_weight: float32 [2, 512, 512], P(None, None, 'chan'), may hold values from -0.25 to 0.25
Outputs:
- updated: float32 [512, 4096], P('chan', 'space')
Inputs may be any that keep to these rules, and one draw needn't show every extreme that they name: `pair_table`: blocks n * 4 to (n + 1) * 4 - 1 lie on device n along space. In slot p of device d's pair slots the first block is one of device d's blocks and the second a block of device (d + o) mod the number of devices along space, with o from 0 to 2; the third row is 0 or 1. On every device the first 3 slots are live and slot o (o = 0 .. 2) names a second block on device d + o; any live slots follow them, empty slots come last.
All inputs are finite; a program needn't handle non-finite values.
Results may differ from a plain program's by a relative error of at most 0.0003.
Values sent between devices are 32-bit elements; how exact they have to be, the bound alone decides.
A program may use at most 64 MiB of HBM per device.

v0:
```python
import jax
import jax.numpy as jnp
from jax import lax
from jax.sharding import PartitionSpec as P

K = 8
LAYERS = 2


cutoff_radius = 6.0
gamma_width = 1.5


def shifted(block, axis, distance):
    devices = range(lax.axis_size(axis))
    route = [((i - distance) % len(devices), i) for i in devices]
    return lax.ppermute(block, axis, route)


def radial_basis(first_geo, second_geo, keep_pair, same_block):
    offsets = first_geo[..., :3, :, None] - second_geo[..., :3, None, :]
    squared = jnp.sum(offsets * offsets, axis=-3)
    distance = jnp.sqrt(squared)
    envelope = jnp.where(
        distance < cutoff_radius, 0.5 * (jnp.cos(jnp.pi * distance / cutoff_radius) + 1.0), 0.0
    )
    extent = distance.shape[-1]
    diagonal = (
        lax.broadcasted_iota(jnp.int32, (extent, extent), 0)
        == lax.broadcasted_iota(jnp.int32, (extent, extent), 1)
    ).astype(jnp.float32)
    allowed = (
        first_geo[..., 3, :, None]
        * second_geo[..., 3, None, :]
        * keep_pair[..., None, None]
        * (1.0 - same_block[..., None, None] * diagonal)
    )
    centers = jnp.arange(K, dtype=jnp.float32) * (cutoff_radius / (K - 1))
    spread = distance[..., None, :, :] - centers[:, None, None]
    return jnp.exp(-gamma_width * spread * spread) * (envelope * allowed)[..., None, :, :]


def to_blocks(stacked, blocks):
    groups, channels, extent = stacked.shape
    shaped = stacked.reshape(groups, channels, blocks, extent // blocks)
    return shaped.transpose(0, 2, 1, 3).reshape(groups * blocks, channels, extent // blocks)


def shards(positions, features, block_counts, pair_table, in_weight, filter_weight, mix_weight):
    spatial = lax.axis_size("space")
    reach_dev = spatial // 4
    own_index = lax.axis_index("space")
    blocks = block_counts.shape[0]
    atoms_dev = positions.shape[1]
    block_len = atoms_dev // blocks
    local_chan = features.shape[0]
    slot_total = (reach_dev + 1) * blocks
    valid = (
        (lax.broadcasted_iota(jnp.int32, (blocks, block_len), 1) < block_counts[:, None])
        .astype(jnp.float32)
        .reshape(1, atoms_dev)
    )
    geometry = jnp.concatenate([positions, valid], axis=0)
    fetched = [geometry]
    for offset in range(1, reach_dev + 1):
        fetched.append(shifted(geometry, "space", -offset))
    geo_blocks = to_blocks(jnp.stack(fetched), blocks)
    first_index = pair_table[0] - own_index * blocks
    second_global = pair_table[1]
    device_ahead = (second_global // blocks - own_index) % spatial
    second_index = device_ahead * blocks + second_global % blocks
    keep_pair = pair_table[2].astype(jnp.float32)
    same_block = (second_index == first_index).astype(jnp.float32)
    per_turn = 2
    turn_count = pair_table.shape[1] // per_turn
    scanned = (
        first_index.reshape(turn_count, per_turn),
        second_index.reshape(turn_count, per_turn),
        keep_pair.reshape(turn_count, per_turn),
        same_block.reshape(turn_count, per_turn),
    )
    state = features
    for layer in range(LAYERS):
        in_rows = in_weight[layer]

        def add_rows(total, segment, first_row, in_rows=in_rows):
            return jnp.dot(
                in_rows,
                segment,
                precision=lax.Precision.HIGHEST,
                preferred_element_type=jnp.float32,
            )

        mapped = add_rows(
            jnp.zeros((local_chan, atoms_dev), jnp.float32),
            lax.all_gather(state, "chan", axis=0, tiled=True),
            jnp.int32(0),
        )
        neighbours = [mapped]
        for offset in range(1, reach_dev + 1):
            neighbours.append(shifted(mapped, "space", -offset))
        feat_blocks = to_blocks(jnp.stack(neighbours), blocks)
        weights_f = filter_weight[layer]

        def pair_turn(collected, inputs, feat_blocks=feat_blocks, weights_f=weights_f):
            first_idx, second_idx, keep_now, same_now = inputs
            basis = radial_basis(geo_blocks[first_idx], geo_blocks[second_idx], keep_now, same_now)
            first_feat = weights_f[None, :, :, None] * feat_blocks[first_idx][:, None]
            second_feat = weights_f[None, :, :, None] * feat_blocks[second_idx][:, None]
            to_first = jnp.einsum(
                "gkcj,gkij->gci", second_feat, basis, precision=lax.Precision.HIGHEST
            )
            to_second = (
                jnp.einsum("gkci,gkij->gcj", first_feat, basis, precision=lax.Precision.HIGHEST)
                * (1.0 - same_now)[:, None, None]
            )
            collected = collected.at[first_idx].add(to_first).at[second_idx].add(to_second)
            return (collected, None)

        collected, unused = lax.scan(
            pair_turn, jnp.zeros((slot_total, local_chan, block_len), jnp.float32), scanned
        )
        received = collected[:blocks]
        for offset in range(1, reach_dev + 1):
            received = received + shifted(
                collected[offset * blocks : (offset + 1) * blocks], "space", offset
            )
        messages = received.transpose(1, 0, 2).reshape(local_chan, atoms_dev)
        mix_cols = mix_weight[layer]

        def mix_rows(start_row, row_count, mix_cols=mix_cols, messages=messages):
            return jnp.dot(
                mix_cols,
                messages,
                precision=lax.Precision.HIGHEST,
                preferred_element_type=jnp.float32,
            )

        own_mixed = lax.psum_scatter(
            mix_rows(jnp.int32(0), local_chan * lax.axis_size("chan")),
            "chan",
            scatter_dimension=0,
            tiled=True,
        )
        state = state + jax.nn.silu(own_mixed)
    return state


def solution(mesh):
    placed = (
        P(None, "space"),
        P("chan", "space"),
        P("space"),
        P(None, "space"),
        P(None, "chan", None),
        P(None, None, "chan"),
        P(None, None, "chan"),
    )
    return jax.shard_map(
        shards, mesh=mesh, in_specs=placed, out_specs=P("chan", "space"), check_vma=False
    )
```

profile of v0, /device:TPU:0, one launch (start us, length us, event | category | flops | bytes accessed | tf_op | source)
XLA Modules:
  0.0 652.5 jit_solution(901403730697041485)
XLA Ops:
  7.4 3.4 collective-permute-start.2
  14.4 25.1 %all-gather.3.cloned.1.call-done = f32[512,512]{1,0:T(8,128)} async-done(((f32[128,512]{1,0:T(8,128)}), f32[512,512]{1,0:T(8,128)}) %all-gather.3.cloned.1.call-update) | async-done | bytes 1048592 | tf_op jit(solution)/shard_map/all_gather | solution.py:96
  39.6 2.0 fusion.62
  41.6 2.4 collective-permute-start.1
  44.1 5.5 collective-permute-done.1
  49.6 2.7 collective-permute-done
  52.6 233.7 %while.24 = (s32[]{:T(128)}, f32[12,128,128]{2,1,0:T(8,128)S(1)}, s32[32,2]{1,0:T(8,128)S(1)}, f32[1,8,128]{2,1,0:T(8,128)S(1)}, s32[32,2]{1,0:T(8,128)S(1)}, /*...) while((s32[]{:T(128)}, f32[12,128,128]{2,1,0:T(8,128)S(1)}, ...), condition=%wide.region_4.5_spmd, body=%wide.region_0.4_spmd.sunk | while | flops 808683520 | bytes 3060089 | solution.py:120
  57.1 1.5 fusion.116
  79.0 1.5 fusion.116
  86.3 1.5 fusion.116
  93.6 1.5 fusion.116
  100.9 1.5 fusion.116
  108.2 1.5 fusion.116
  122.8 1.5 fusion.116
  130.1 1.5 fusion.116
  195.8 1.5 fusion.116
  268.9 1.5 fusion.116
  286.6 2.3 collective-permute-start.5
  288.9 6.7 %collective-permute-done.4 = f32[4,128,128]{1,2,0:T(8,128)S(1)} collective-permute-done((f32[4,128,128]{1,2,0:T(8,128)S(1)}, f32[4,128,128]{1,2,0:T(8,128)S(1)}, u32[]{:S(2)}, u32[]{:S(2)}) %collective-permute-start.4) | collective-permute-done | bytes 262176 | tf_op jit(solution)/shard_map/ppermute | solution.py:17
  297.0 2.0 convolution_bitcast_fusion.5
  300.1 25.8 %reduce-scatter.3.cloned.1.call-done = f32[128,512]{0,1:T(8,128)} async-done(((f32[512,512]{0,1:T(8,128)}), f32[128,512]{0,1:T(8,128)}) %reduce-scatter.3.cloned.1.call-update) | async-done | bytes 262160 | tf_op jit(solution)/shard_map/reduce_scatter | solution.py:139
  325.9 1.7 multiply_add_fusion.1
  327.7 29.0 %all-gather.5.cloned.1.call-done = f32[512,512]{0,1:T(8,128)} async-done(((f32[128,512]{0,1:T(8,128)}), f32[512,512]{0,1:T(8,128)}) %all-gather.5.cloned.1.call-update) | async-done | bytes 1048592 | tf_op jit(solution)/shard_map/all_gather | solution.py:96
  356.7 2.4 fusion.59
  360.8 6.0 collective-permute-done.6
  366.8 2.8 collective-permute-done.7
  369.8 233.6 %while.25 = (s32[]{:T(128)}, f32[12,128,128]{2,1,0:T(8,128)S(1)}, s32[32,2]{1,0:T(8,128)S(1)}, f32[1,8,128]{2,1,0:T(8,128)S(1)}, s32[32,2]{1,0:T(8,128)S(1)}, /*...) while((s32[]{:T(128)}, f32[12,128,128]{2,1,0:T(8,128)S(1)}, ...), condition=%wide.region_10.11_spmd, body=%wide.region_6.10_spmd.sunk | while | flops 808683520 | bytes 3060089 | solution.py:120
  603.9 2.5 collective-permute-start.9
  606.4 5.9 collective-permute-done.8
  612.3 2.2 collective-permute-done.9
  614.5 2.0 convolution_bitcast_fusion.4
  616.5 27.6 %reduce-scatter.5.cloned.1.call-done = f32[128,512]{0,1:T(8,128)} async-done(((f32[512,512]{0,1:T(8,128)}), f32[128,512]{0,1:T(8,128)}) %reduce-scatter.5.cloned.1.call-update) | async-done | bytes 262160 | tf_op jit(solution)/shard_map/reduce_scatter | solution.py:139
  (1269 shorter events, 457.0 us)
Async XLA Ops:
  6.5 0.8 copy-start.6
  6.5 33.1 %all-gather.3.cloned.1.call-start = ((), (), s32[]{:S(2)}) async-start(), calls=%async_computation.2 | async-start | bytes 1310720 | tf_op jit(solution)/shard_map/all_gather | solution.py:96
  6.5 0.8 copy-start.4
  7.3 318.6 %reduce-scatter.3.cloned.1.call-start = ((), (), s32[]{:S(2)}) async-start(), calls=%async_computation.3 | async-start | bytes 1310720 | tf_op jit(solution)/shard_map/reduce_scatter | solution.py:139
  7.4 5.8 collective-permute-start.2
  10.8 3.7 collective-permute-start.3
  11.4 0.7 copy-start.7
  12.3 0.7 copy-start.5
  41.6 8.0 %collective-permute-start.1 = (f32[128,512]{1,0:T(8,128)S(1)}, f32[128,512]{1,0:T(8,128)S(1)}, u32[]{:S(2)}, u32[]{:S(2)}) collective-permute-start(f32[128,512]{1,0:T(8,128)S(1)} %fusion.62), channel_id=1, source_target_pairs={{8,0},{12,4},{16,8},{20,12},{24,16},{28,20},{0,24},{4,28},{9,1},{1... | collective-permute-start | bytes 786440 | tf_op jit(solution)/shard_map/ppermute | solution.py:17
  44.1 8.2 %collective-permute-start = (f32[128,512]{1,0:T(8,128)S(1)}, f32[128,512]{1,0:T(8,128)S(1)}, u32[]{:S(2)}, u32[]{:S(2)}) collective-permute-start(f32[128,512]{1,0:T(8,128)S(1)} %fusion.62), channel_id=1, source_target_pairs={{4,0},{8,4},{12,8},{16,12},{20,16},{24,20},{28,24},{0,28},{5,1},{9... | collective-permute-start | bytes 786440 | tf_op jit(solution)/shard_map/ppermute | solution.py:17
  286.6 9.1 %collective-permute-start.4 = (f32[4,128,128]{1,2,0:T(8,128)S(1)}, f32[4,128,128]{1,2,0:T(8,128)S(1)}, u32[]{:S(2)}, u32[]{:S(2)}) collective-permute-start(f32[4,128,128]{1,2,0:T(8,128)S(1)} %get-tuple-element.291), channel_id=1, source_target_pairs={{28,0},{0,4},{4,8},{8,12},{12,16},{16,20},{20,24},{24,28},{29,1},{... | collective-permute-start | bytes 786440 | tf_op jit(solution)/shard_map/ppermute | solution.py:17
  286.6 10.4 %copy-start.3 = (f32[2,512,128]{2,1,0:T(8,128)S(1)}, f32[2,512,128]{2,1,0:T(8,128)}, u32[]{:S(2)}) copy-start(f32[2,512,128]{2,1,0:T(8,128)} %param.17) | copy-start | bytes 1572868
  286.6 10.3 %collective-permute-start.5 = (f32[4,128,128]{1,2,0:T(8,128)S(1)}, f32[4,128,128]{1,2,0:T(8,128)S(1)}, u32[]{:S(2)}, u32[]{:S(2)}) collective-permute-start(f32[4,128,128]{1,2,0:T(8,128)S(1)} %get-tuple-element.292), channel_id=1, source_target_pairs={{24,0},{28,4},{0,8},{4,12},{8,16},{12,20},{16,24},{20,28},{25,1},{... | collective-permute-start | bytes 786440 | tf_op jit(solution)/shard_map/ppermute | solution.py:17
  299.0 0.9 copy-start.1
  299.0 57.7 %all-gather.5.cloned.1.call-start = ((), (), s32[]{:S(2)}) async-start(), calls=%async_computation.4 | async-start | bytes 1310720 | tf_op jit(solution)/shard_map/all_gather | solution.py:96
  300.0 56.6 %copy-start.2 = (f32[2,128,512]{2,1,0:T(8,128)S(1)}, f32[2,128,512]{2,1,0:T(8,128)}, u32[]{:S(2)}) copy-start(f32[2,128,512]{2,1,0:T(8,128)} %param.15) | copy-start | bytes 1572868
  327.6 316.5 %reduce-scatter.5.cloned.1.call-start = ((), (), s32[]{:S(2)}) async-start(), calls=%async_computation.5 | async-start | bytes 1310720 | tf_op jit(solution)/shard_map/reduce_scatter | solution.py:139
  359.1 7.7 %collective-permute-start.6 = (f32[128,512]{1,0:T(8,128)S(1)}, f32[128,512]{1,0:T(8,128)S(1)}, u32[]{:S(2)}, u32[]{:S(2)}) collective-permute-start(f32[128,512]{1,0:T(8,128)S(1)} %bitcast.153), channel_id=1, source_target_pairs={{4,0},{8,4},{12,8},{16,12},{20,16},{24,20},{28,24},{0,28},{5,1},{9... | collective-permute-start | bytes 786440 | tf_op jit(solution)/shard_map/ppermute | solution.py:17
  360.2 9.4 %collective-permute-start.7 = (f32[128,512]{1,0:T(8,128)S(1)}, f32[128,512]{1,0:T(8,128)S(1)}, u32[]{:S(2)}, u32[]{:S(2)}) collective-permute-start(f32[128,512]{1,0:T(8,128)S(1)} %bitcast.154), channel_id=1, source_target_pairs={{8,0},{12,4},{16,8},{20,12},{24,16},{28,20},{0,24},{4,28},{9,1},{1... | collective-permute-start | bytes 786440 | tf_op jit(solution)/shard_map/ppermute | solution.py:17
  603.8 8.5 %collective-permute-start.8 = (f32[4,128,128]{1,2,0:T(8,128)S(1)}, f32[4,128,128]{1,2,0:T(8,128)S(1)}, u32[]{:S(2)}, u32[]{:S(2)}) collective-permute-start(f32[4,128,128]{1,2,0:T(8,128)S(1)} %get-tuple-element.285), channel_id=1, source_target_pairs={{28,0},{0,4},{4,8},{8,12},{12,16},{16,20},{20,24},{24,28},{29,1},{... | collective-permute-start | bytes 786440 | tf_op jit(solution)/shard_map/ppermute | solution.py:17
  603.9 10.6 %collective-permute-start.9 = (f32[4,128,128]{1,2,0:T(8,128)S(1)}, f32[4,128,128]{1,2,0:T(8,128)S(1)}, u32[]{:S(2)}, u32[]{:S(2)}) collective-permute-start(f32[4,128,128]{1,2,0:T(8,128)S(1)} %get-tuple-element.286), channel_id=1, source_target_pairs={{24,0},{28,4},{0,8},{4,12},{8,16},{12,20},{16,24},{20,28},{25,1},{... | collective-permute-start | bytes 786440 | tf_op jit(solution)/shard_map/ppermute | solution.py:17
  616.5 27.6 %copy-start = (f32[128,512]{0,1:T(8,128)S(1)}, f32[128,512]{0,1:T(8,128)}, u32[]{:S(2)}) copy-start(f32[128,512]{0,1:T(8,128)} %multiply_add_fusion.1) | copy-start | bytes 786436
Sparse Core Ops, SparseCore 0:
  8.9 30.6 all-gather.2
  299.1 26.7 reduce-scatter.2
  327.8 28.8 all-gather.4
  616.6 27.4 reduce-scatter.4
where the time goes:
time: 653 us; the launch traced here: 652 us
  matrix products  192 us (29%)
  local copies, waits for them, and re-layouts  150 us (23%)
  waiting for transfers between devices  143 us (22%)
  other arithmetic  133 us (20%)
  between operations  13.4 us (2%)
  starting transfers between devices  13.1 us (2%)
  loops' own time  7.17 us (1%)
    dot_general x64, matrix products, pair_turn(): jnp.einsum('gkci,gkij->gcj', first_feat, basis, precision=lax.Precision.H...  94.9 us
    dot_general x64, matrix products, pair_turn(): jnp.einsum('gkcj,gkij->gci', second_feat, basis, precision=lax.Precision....  89.1 us
    scatter-add x128, other arithmetic, pair_turn(): collected.at[first_idx].add(to_first).at[second_idx].add(to_second)  81.9 us
    all_gather x2, waiting for transfers between devices, shards(): lax.all_gather(state, 'chan', axis=0, tiled=True)  54.1 us
    reduce_scatter x2, waiting for transfers between devices, shards(): lax.psum_scatter(mix_rows(jnp.int32(0), local_chan * lax.axis_size('chan'...  53.4 us
    gather x64, local copies, waits for them, and re-layouts, pair_turn(): geo_blocks[second_idx]  36.5 us
    gather x64, local copies, waits for them, and re-layouts, pair_turn(): geo_blocks[first_idx]  36.5 us
    gather x64, local copies, waits for them, and re-layouts, pair_turn(): second_feat = weights_f[None, :, :, None] * feat_blocks[second_idx][:, None]  35.8 us
  transfers between devices with their start and end apart: 14, of which 13 were waited for; matrix products, arithmetic and copies ran while one was open for 0% of the time, Pallas kernels for 0%

commit v1 on v0

v1 whole, which is shorter than its diff:
```python
import functools
import math

import jax
import jax.numpy as jnp
from jax import lax
from jax.experimental import pallas as pl
from jax.experimental.pallas import tpu as pltpu
from jax.sharding import PartitionSpec as P

K = 8
LAYERS = 2


cutoff_radius = 6.0
gamma_width = 1.5
spacing = cutoff_radius / (K - 1)


def shifted(block, axis, distance):
    devices = range(lax.axis_size(axis))
    route = [((i - distance) % len(devices), i) for i in devices]
    return lax.ppermute(block, axis, route)


def half_cosine(y):
    terms = [(-1) ** n * (math.pi / 2) ** (2 * n) / math.factorial(2 * n) for n in range(8)]
    total = jnp.full_like(y, terms[-1])
    for term in terms[-2::-1]:
        total = total * y + term
    return total


def split_halves(value):
    high = value.astype(jnp.bfloat16)
    low = (value - high.astype(jnp.float32)).astype(jnp.bfloat16)
    return high, low


def write_basis(columns, rows, weight, same, out):
    squared = 0.0
    for axis in range(3):
        offset = columns[:, axis : axis + 1] - rows[axis : axis + 1, :]
        squared = squared + offset * offset
    extent = squared.shape[0]
    limit = cutoff_radius * cutoff_radius
    near = jnp.minimum(squared, limit)
    distance = jnp.sqrt(near)
    root = half_cosine(near * (1.0 / limit))
    allowed = (columns[:, 3:4] * weight) * rows[3:4, :]
    diagonal = lax.broadcasted_iota(jnp.int32, (extent, extent), 0) == lax.broadcasted_iota(
        jnp.int32, (extent, extent), 1
    )
    dropped = (squared >= limit) | (diagonal & same)
    envelope = jnp.where(dropped, 0.0, root * root * allowed)
    middle = K // 2 - 1
    spread = distance - middle * spacing
    centre = jnp.exp(-gamma_width * spread * spread) * envelope
    slope = 2.0 * gamma_width * spacing
    up = jnp.exp(slope * distance)
    down = jnp.exp(-slope * distance)

    def put(k, value):
        high, low = split_halves(value)
        out[k * extent : (k + 1) * extent, :extent] = high
        out[k * extent : (k + 1) * extent, extent:] = low

    put(middle, centre)
    unit = gamma_width * spacing * spacing
    value = centre
    for k in range(middle + 1, K):
        value = value * (up * math.exp(-unit * (2 * k - 1)))
        put(k, value)
    value = centre
    for k in range(middle - 1, -1, -1):
        value = value * (down * math.exp(unit * (2 * k + 1)))
        put(k, value)


def pair_kernel(
    blocks,
    base_ref,
    table_ref,
    columns_ref,
    rows_ref,
    mapped_ref,
    filter_ref,
    out_ref,
    count_s,
    to_s,
    from_s,
    weight_s,
    operand_v,
    basis_a,
    basis_b,
):
    slots, extent, channels = mapped_ref.shape
    spatial = base_ref[1]
    own = base_ref[0]

    def clear(i, carry):
        count_s[i] = 0
        return carry

    lax.fori_loop(0, blocks * slots, clear, 0)

    def tally(p, carry):
        first = table_ref[0, p] - own * blocks
        second = table_ref[1, p]
        holder = second // blocks
        ahead = holder - own
        ahead = jnp.where(ahead < 0, ahead + spatial, ahead)
        second = ahead * blocks + (second - holder * blocks)
        swap = second < first
        at = jnp.where(swap, second, first) * slots + jnp.where(swap, first, second)
        count_s[at] = count_s[at] + table_ref[2, p]
        return carry

    lax.fori_loop(0, table_ref.shape[1], tally, 0)

    def list_row(first, n):
        def list_one(second, n):
            many = count_s[first * slots + second]
            live = (many > 0).astype(jnp.int32)
            other = live * (first != second).astype(jnp.int32)
            weight = many.astype(jnp.float32)
            to_s[n] = first
            from_s[n] = second
            weight_s[n] = weight
            n = n + live
            to_s[n] = second
            from_s[n] = first
            weight_s[n] = weight
            return n + other

        return lax.fori_loop(first, slots, list_one, n)

    total = lax.fori_loop(0, blocks, list_row, 0)
    for extra in range(3):
        to_s[total + extra] = 0
        from_s[total + extra] = 0
        weight_s[total + extra] = 0.0

    for slot in range(slots):
        high, low = split_halves(mapped_ref[slot])
        for part in range(2):
            operand_v[slot, part * extent : (part + 1) * extent, :channels] = high
            operand_v[slot, part * extent : (part + 1) * extent, channels:] = low
    out_ref[...] = jnp.zeros_like(out_ref)

    def build(task, basis):
        to, source = to_s[task], from_s[task]
        write_basis(columns_ref[to], rows_ref[source], weight_s[task], to == source, basis)

    def spend(task, basis):
        to, source = to_s[task], from_s[task]
        product = jnp.dot(basis[...], operand_v[source], preferred_element_type=jnp.float32)
        summed = 0.0
        for k in range(K):
            part = product[k * extent : (k + 1) * extent]
            summed = summed + filter_ref[k : k + 1, :] * (part[:, :channels] + part[:, channels:])
        out_ref[to] = out_ref[to] + summed

    build(0, basis_a)

    def step(turn, carry):
        task = 2 * turn
        build(task + 1, basis_b)
        spend(task, basis_a)
        build(task + 2, basis_a)
        spend(task + 1, basis_b)
        return carry

    lax.fori_loop(0, (total + 1) // 2, step, 0)


def pair_messages(base, table, columns, rows, mapped, filters, blocks, interpret=False):
    slots, extent, channels = mapped.shape
    tasks = 2 * blocks * slots + 8
    smem = pl.BlockSpec(memory_space=pltpu.SMEM)
    vmem = pl.BlockSpec(memory_space=pltpu.VMEM)
    return pl.pallas_call(
        functools.partial(pair_kernel, blocks),
        out_shape=jax.ShapeDtypeStruct(mapped.shape, jnp.float32),
        in_specs=[smem, smem, vmem, vmem, vmem, vmem],
        out_specs=vmem,
        scratch_shapes=[
            pltpu.SMEM((blocks * slots,), jnp.int32),
            pltpu.SMEM((tasks,), jnp.int32),
            pltpu.SMEM((tasks,), jnp.int32),
            pltpu.SMEM((tasks,), jnp.float32),
            pltpu.VMEM((slots, 2 * extent, 2 * channels), jnp.bfloat16),
            pltpu.VMEM((K * extent, 2 * extent), jnp.bfloat16),
            pltpu.VMEM((K * extent, 2 * extent), jnp.bfloat16),
        ],
        compiler_params=pltpu.CompilerParams(vmem_limit_bytes=48 * 1024 * 1024),
        interpret=interpret,
    )(base, table, columns, rows, mapped, filters)


def shards(positions, features, block_counts, pair_table, in_weight, filter_weight, mix_weight):
    spatial = lax.axis_size("space")
    reach_dev = spatial // 4
    own_index = lax.axis_index("space")
    blocks = block_counts.shape[0]
    atoms_dev = positions.shape[1]
    block_len = atoms_dev // blocks
    local_chan = features.shape[0]
    slot_total = (reach_dev + 1) * blocks
    valid = (
        (lax.broadcasted_iota(jnp.int32, (blocks, block_len), 1) < block_counts[:, None])
        .astype(jnp.float32)
        .reshape(1, atoms_dev)
    )
    geometry = jnp.concatenate([positions, valid, jnp.zeros((4, atoms_dev), jnp.float32)], axis=0)
    fetched = [geometry]
    for offset in range(1, reach_dev + 1):
        fetched.append(shifted(geometry, "space", -offset))
    rows = jnp.concatenate(
        [part.reshape(8, blocks, block_len).transpose(1, 0, 2) for part in fetched], axis=0
    )
    columns = rows.transpose(0, 2, 1)
    base = jnp.stack([own_index, jnp.int32(spatial)]).astype(jnp.int32)
    state = features
    for layer in range(LAYERS):
        full_state = lax.all_gather(state, "chan", axis=0, tiled=True)
        mapped = lax.dot_general(
            full_state,
            in_weight[layer],
            (((0,), (1,)), ((), ())),
            precision=lax.Precision.HIGHEST,
            preferred_element_type=jnp.float32,
        )
        neighbours = [mapped]
        for offset in range(1, reach_dev + 1):
            neighbours.append(shifted(mapped, "space", -offset))
        mapped_blocks = jnp.concatenate(neighbours, axis=0).reshape(slot_total, block_len, local_chan)
        collected = pair_messages(
            base, pair_table, columns, rows, mapped_blocks, filter_weight[layer], blocks
        ).reshape(reach_dev + 1, atoms_dev, local_chan)
        received = collected[0]
        for offset in range(1, reach_dev + 1):
            received = received + shifted(collected[offset], "space", offset)
        mixed = lax.dot_general(
            mix_weight[layer],
            received,
            (((1,), (1,)), ((), ())),
            precision=lax.Precision.HIGHEST,
            preferred_element_type=jnp.float32,
        )
        own_mixed = lax.psum_scatter(mixed, "chan", scatter_dimension=0, tiled=True)
        state = state + jax.nn.silu(own_mixed)
    return state


def solution(mesh):
    placed = (
        P(None, "space"),
        P("chan", "space"),
        P("space"),
        P(None, "space"),
        P(None, "chan", None),
        P(None, None, "chan"),
        P(None, None, "chan"),
    )
    return jax.shard_map(
        shards, mesh=mesh, in_specs=placed, out_specs=P("chan", "space"), check_vma=False
    )
```

time: 653 us -> 237 us (0.36)
  matrix products: 192 us -> 9.27 us
  local copies, waits for them, and re-layouts: 150 us -> 4.46 us
  other arithmetic: 133 us -> 3.31 us
  Pallas kernels: 0 us -> 44 us
  loops' own time: 7.17 us -> 0 us
    dot_general x132 -> x4, matrix products: 192 us -> 9.27 us  [the longest x2 5.27 us: shards(): lax.dot_general(full_state, in_weight[layer], (((0,), (1,)), ((), ())), p...]
    gather x256 -> x0, local copies, waits for them, and re-layouts: 144 us -> none  [the longest x64 36.5 us: pair_turn(): geo_blocks[second_idx]]
    scatter-add x128 -> x0, other arithmetic: 81.9 us -> none  [pair_turn(): collected.at[first_idx].add(to_first).at[second_idx].add(to_second)]
    pallas_call x0 -> x2, Pallas kernels: none -> 44 us  [pair_messages(): pl.pallas_call(functools.partial(pair_kernel, blocks), out_shape=jax.Shap...]
    sqrt x64 -> x0, other arithmetic: 33.8 us -> none  [radial_basis(): distance = jnp.sqrt(squared)]
    reduce_sum x64 -> x0, other arithmetic: 10.8 us -> none  [radial_basis(): squared = jnp.sum(offsets * offsets, axis=-3)]
    another operation x2 -> x0, loops' own time: 7.17 us -> none  [shards(): lax.scan(pair_turn, jnp.zeros((slot_total, local_chan, block_len), jnp.fl...]
  transfers between devices with their start and end apart: 14 -> 14, of which waited for: 13 -> 12; matrix products, arithmetic and copies ran while one was open for 0% -> 2% of each run, Pallas kernels for 0% -> 0%
where the time goes in v1:
time: 237 us; the launch traced here: 236 us
  waiting for transfers between devices  142 us (60%)
  Pallas kernels  44 us (19%)
  starting transfers between devices  19.4 us (8%)
  between operations  13.3 us (6%)
  matrix products  9.27 us (4%)
  local copies, waits for them, and re-layouts  4.46 us (2%)
  other arithmetic  3.31 us (1%)
    all_gather x2, waiting for transfers between devices, shards(): full_state = lax.all_gather(state, 'chan', axis=0, tiled=True)  56.4 us
    reduce_scatter x2, waiting for transfers between devices, shards(): own_mixed = lax.psum_scatter(mixed, 'chan', scatter_dimension=0, tiled=True)  54.1 us
    pallas_call x2, Pallas kernels, pair_messages(): pl.pallas_call(functools.partial(pair_kernel, blocks), out_shape=jax.Shap...  44 us
    ppermute x10, waiting for transfers between devices, shifted(): return lax.ppermute(block, axis, route)  31 us
    ppermute x10, starting transfers between devices, shifted(): return lax.ppermute(block, axis, route)  19.3 us
    dot_general x2, matrix products, shards(): lax.dot_general(full_state, in_weight[layer], (((0,), (1,)), ((), ())), p...  5.27 us
  transfers between devices with their start and end apart: 14, of which 12 were waited for; matrix products, arithmetic and copies ran while one was open for 2% of the time, Pallas kernels for 0%

profile of v1, /device:TPU:0, one launch (start us, length us, event | category | flops | bytes accessed | tf_op | source)
XLA Modules:
  0.0 236.0 jit_solution(17792904279903550932)
XLA Ops:
  6.5 0.7 all-gather.3.cloned.1.call-update
  8.0 3.3 %collective-permute-start = (f32[8,512]{1,0:T(8,128)S(1)}, f32[8,512]{1,0:T(8,128)S(1)}, u32[]{:S(2)}, u32[]{:S(2)}) collective-permute-start(f32[8,512]{1,0:T(8,128)S(1)} %maximum_maximum_fusion), channel_id=1, source_target_pairs={{4,0},{8,4},{12,8},{16,12},{20,16},{24,20},{28,24},{0,28},{5,1},{9... | collective-permute-start | bytes 49160 | tf_op jit(solution)/shard_map/ppermute | solution.py:23
  11.4 0.6 collective-permute-start.1
  12.1 27.5 %all-gather.3.cloned.1.call-done = f32[512,512]{1,0:T(8,128)} async-done(((f32[128,512]{1,0:T(8,128)}), f32[512,512]{1,0:T(8,128)}) %all-gather.3.cloned.1.call-update) | async-done | bytes 1048592 | tf_op jit(solution)/shard_map/all_gather | solution.py:226
  39.6 3.1 %fusion.6 = f32[512,128]{1,0:T(8,128)S(1)} fusion(f32[512,512]{1,0:T(8,128)} %all-gather.3.cloned.1.call-done, f32[2,128,512]{2,1,0:T(8,128)} %param.11), kind=kOutput, calls=%fused_computation.12 | convolution fusion | flops 402653184 | bytes 1572864 | tf_op jit(solution)/shard_map/dot_general | solution.py:227
  42.7 1.7 collective-permute-start.2
  44.4 0.8 collective-permute-start.3
  45.5 5.3 %collective-permute-done.2 = f32[512,128]{1,0:T(8,128)S(1)} collective-permute-done((f32[512,128]{1,0:T(8,128)S(1)}, f32[512,128]{1,0:T(8,128)S(1)}, u32[]{:S(2)}, u32[]{:S(2)}) %collective-permute-start.2) | collective-permute-done | bytes 262176 | tf_op jit(solution)/shard_map/ppermute | solution.py:23
  50.9 3.3 %collective-permute-done.3 = f32[512,128]{1,0:T(8,128)S(1)} collective-permute-done((f32[512,128]{1,0:T(8,128)S(1)}, f32[512,128]{1,0:T(8,128)S(1)}, u32[]{:S(2)}, u32[]{:S(2)}) %collective-permute-start.3) | collective-permute-done | bytes 262176 | tf_op jit(solution)/shard_map/ppermute | solution.py:23
  54.2 0.7 copy-done
  54.9 22.0 %shard_map.73 = f32[12,128,128]{2,1,0:T(8,128)S(1)} custom-call(s32[2]{0:T(128)S(1)} %pad_add_fusion.base_ref, s32[3,64]{1,0:T(4,128)S(1)} %copy-done, f32[12,128,8]{2,1,0:T(8,128)S(1)} %copy.8.columns_ref, f32[12,8,128]{2,1,0:T(8,128)S(1)} %get-tuple-element.11.rows_ref, f32[12,128,128]{2,1,0:T(8,128)S(1)} %bitcast.52, ...), custom_call_target="tpu_custom_call" | custom-call | tf_op jit(solution)/shard_map/pallas_call | solution.py:182
  77.0 5.7 %collective-permute-start.5 = (f32[512,128]{1,0:T(8,128)S(1)}, f32[512,128]{1,0:T(8,128)S(1)}, u32[]{:S(2)}, u32[]{:S(2)}) collective-permute-start(f32[512,128]{1,0:T(8,128)S(1)} %bitcast.53), channel_id=1, source_target_pairs={{24,0},{28,4},{0,8},{4,12},{8,16},{12,20},{16,24},{20,28},{25,1},{... | collective-permute-start | bytes 786440 | tf_op jit(solution)/shard_map/ppermute | solution.py:23
  82.7 3.2 %collective-permute-done.4 = f32[512,128]{1,0:T(8,128)S(1)} collective-permute-done((f32[512,128]{1,0:T(8,128)S(1)}, f32[512,128]{1,0:T(8,128)S(1)}, u32[]{:S(2)}, u32[]{:S(2)}) %collective-permute-start.4) | collective-permute-done | bytes 262176 | tf_op jit(solution)/shard_map/ppermute | solution.py:23
  86.0 3.5 %collective-permute-done.5 = f32[512,128]{1,0:T(8,128)S(1)} collective-permute-done((f32[512,128]{1,0:T(8,128)S(1)}, f32[512,128]{1,0:T(8,128)S(1)}, u32[]{:S(2)}, u32[]{:S(2)}) %collective-permute-start.5) | collective-permute-done | bytes 262176 | tf_op jit(solution)/shard_map/ppermute | solution.py:23
  89.5 1.0 copy-done.4
  90.5 2.0 convolution_bitcast_fusion.1
  92.6 0.9 copy-done.2
  93.6 26.8 %reduce-scatter.3.cloned.1.call-done = f32[128,512]{0,1:T(8,128)} async-done(((f32[512,512]{0,1:T(8,128)}), f32[128,512]{0,1:T(8,128)}) %reduce-scatter.3.cloned.1.call-update) | async-done | bytes 262160 | tf_op jit(solution)/shard_map/reduce_scatter | solution.py:251
  120.4 1.7 multiply_add_fusion.1
  122.2 29.0 %all-gather.5.cloned.1.call-done = f32[512,512]{0,1:T(8,128)} async-done(((f32[128,512]{0,1:T(8,128)}), f32[512,512]{0,1:T(8,128)}) %all-gather.5.cloned.1.call-update) | async-done | bytes 1048592 | tf_op jit(solution)/shard_map/all_gather | solution.py:226
  151.2 2.2 fusion.2
  153.4 1.1 collective-permute-start.6
  155.0 6.0 %collective-permute-done.6 = f32[512,128]{1,0:T(8,128)S(1)} collective-permute-done((f32[512,128]{1,0:T(8,128)S(1)}, f32[512,128]{1,0:T(8,128)S(1)}, u32[]{:S(2)}, u32[]{:S(2)}) %collective-permute-start.6) | collective-permute-done | bytes 262176 | tf_op jit(solution)/shard_map/ppermute | solution.py:23
  161.1 2.8 %collective-permute-done.7 = f32[512,128]{1,0:T(8,128)S(1)} collective-permute-done((f32[512,128]{1,0:T(8,128)S(1)}, f32[512,128]{1,0:T(8,128)S(1)}, u32[]{:S(2)}, u32[]{:S(2)}) %collective-permute-start.7) | collective-permute-done | bytes 262176 | tf_op jit(solution)/shard_map/ppermute | solution.py:23
  163.9 22.0 %shard_map.74 = f32[12,128,128]{2,1,0:T(8,128)S(1)} custom-call(s32[2]{0:T(128)S(1)} %pad_add_fusion.base_ref, s32[3,64]{1,0:T(4,128)S(1)} %copy-done, f32[12,128,8]{2,1,0:T(8,128)S(1)} %copy.8.columns_ref, f32[12,8,128]{2,1,0:T(8,128)S(1)} %get-tuple-element.11.rows_ref, f32[12,128,128]{2,1,0:T(8,128)S(1)} %bitcast.51, ...), custom_call_target="tpu_custom_call" | custom-call | tf_op jit(solution)/shard_map/pallas_call | solution.py:182
  186.1 5.4 %collective-permute-start.9 = (f32[512,128]{1,0:T(8,128)S(1)}, f32[512,128]{1,0:T(8,128)S(1)}, u32[]{:S(2)}, u32[]{:S(2)}) collective-permute-start(f32[512,128]{1,0:T(8,128)S(1)} %bitcast.54), channel_id=1, source_target_pairs={{24,0},{28,4},{0,8},{4,12},{8,16},{12,20},{16,24},{20,28},{25,1},{... | collective-permute-start | bytes 786440 | tf_op jit(solution)/shard_map/ppermute | solution.py:23
  191.5 3.5 %collective-permute-done.8 = f32[512,128]{1,0:T(8,128)S(1)} collective-permute-done((f32[512,128]{1,0:T(8,128)S(1)}, f32[512,128]{1,0:T(8,128)S(1)}, u32[]{:S(2)}, u32[]{:S(2)}) %collective-permute-start.8) | collective-permute-done | bytes 262176 | tf_op jit(solution)/shard_map/ppermute | solution.py:23
  195.0 3.2 %collective-permute-done.9 = f32[512,128]{1,0:T(8,128)S(1)} collective-permute-done((f32[512,128]{1,0:T(8,128)S(1)}, f32[512,128]{1,0:T(8,128)S(1)}, u32[]{:S(2)}, u32[]{:S(2)}) %collective-permute-start.9) | collective-permute-done | bytes 262176 | tf_op jit(solution)/shard_map/ppermute | solution.py:23
  198.3 2.0 convolution_bitcast_fusion
  200.3 27.3 %reduce-scatter.5.cloned.1.call-done = f32[128,512]{0,1:T(8,128)} async-done(((f32[512,512]{0,1:T(8,128)}), f32[128,512]{0,1:T(8,128)}) %reduce-scatter.5.cloned.1.call-update) | async-done | bytes 262160 | tf_op jit(solution)/shard_map/reduce_scatter | solution.py:251
  227.6 1.0 multiply_add_fusion
  228.6 0.8 copy.11
  (42 shorter events, 2.5 us)
Async XLA Ops:
  6.5 33.1 %all-gather.3.cloned.1.call-start = ((), (), s32[]{:S(2)}) async-start(), calls=%async_computation.2 | async-start | bytes 1310720 | tf_op jit(solution)/shard_map/all_gather | solution.py:226
  6.5 0.9 copy-start.7
  7.3 0.7 copy-start.5
  7.3 113.1 %reduce-scatter.3.cloned.1.call-start = ((), (), s32[]{:S(2)}) async-start(), calls=%async_computation.3 | async-start | bytes 1310720 | tf_op jit(solution)/shard_map/reduce_scatter | solution.py:251
  8.0 37.2 %collective-permute-start = (f32[8,512]{1,0:T(8,128)S(1)}, f32[8,512]{1,0:T(8,128)S(1)}, u32[]{:S(2)}, u32[]{:S(2)}) collective-permute-start(f32[8,512]{1,0:T(8,128)S(1)} %maximum_maximum_fusion), channel_id=1, source_target_pairs={{4,0},{8,4},{12,8},{16,12},{20,16},{24,20},{28,24},{0,28},{5,1},{9... | collective-permute-start | bytes 49160 | tf_op jit(solution)/shard_map/ppermute | solution.py:23
  11.4 33.9 %collective-permute-start.1 = (f32[8,512]{1,0:T(8,128)S(1)}, f32[8,512]{1,0:T(8,128)S(1)}, u32[]{:S(2)}, u32[]{:S(2)}) collective-permute-start(f32[8,512]{1,0:T(8,128)S(1)} %maximum_maximum_fusion), channel_id=1, source_target_pairs={{8,0},{12,4},{16,8},{20,12},{24,16},{28,20},{0,24},{4,28},{9,1},{1... | collective-permute-start | bytes 49160 | tf_op jit(solution)/shard_map/ppermute | solution.py:23
  12.1 33.0 %copy-start.6 = (f32[2,8,128]{2,1,0:T(8,128)S(1)}, f32[2,8,128]{2,1,0:T(8,128)}, u32[]{:S(2)}) copy-start(f32[2,8,128]{2,1,0:T(8,128)} %param.12) | copy-start | bytes 24580
  42.7 8.2 %collective-permute-start.2 = (f32[512,128]{1,0:T(8,128)S(1)}, f32[512,128]{1,0:T(8,128)S(1)}, u32[]{:S(2)}, u32[]{:S(2)}) collective-permute-start(f32[512,128]{1,0:T(8,128)S(1)} %fusion.6), channel_id=1, source_target_pairs={{4,0},{8,4},{12,8},{16,12},{20,16},{24,20},{28,24},{0,28},{5,1},{9... | collective-permute-start | bytes 786440 | tf_op jit(solution)/shard_map/ppermute | solution.py:23
  44.4 9.8 %collective-permute-start.3 = (f32[512,128]{1,0:T(8,128)S(1)}, f32[512,128]{1,0:T(8,128)S(1)}, u32[]{:S(2)}, u32[]{:S(2)}) collective-permute-start(f32[512,128]{1,0:T(8,128)S(1)} %fusion.6), channel_id=1, source_target_pairs={{8,0},{12,4},{16,8},{20,12},{24,16},{28,20},{0,24},{4,28},{9,1},{1... | collective-permute-start | bytes 786440 | tf_op jit(solution)/shard_map/ppermute | solution.py:23
  54.2 0.7 copy-start
  77.0 9.0 %collective-permute-start.4 = (f32[512,128]{1,0:T(8,128)S(1)}, f32[512,128]{1,0:T(8,128)S(1)}, u32[]{:S(2)}, u32[]{:S(2)}) collective-permute-start(f32[512,128]{1,0:T(8,128)S(1)} %bitcast.55), channel_id=1, source_target_pairs={{28,0},{0,4},{4,8},{8,12},{12,16},{16,20},{20,24},{24,28},{29,1},{... | collective-permute-start | bytes 786440 | tf_op jit(solution)/shard_map/ppermute | solution.py:23
  77.0 12.4 %collective-permute-start.5 = (f32[512,128]{1,0:T(8,128)S(1)}, f32[512,128]{1,0:T(8,128)S(1)}, u32[]{:S(2)}, u32[]{:S(2)}) collective-permute-start(f32[512,128]{1,0:T(8,128)S(1)} %bitcast.53), channel_id=1, source_target_pairs={{24,0},{28,4},{0,8},{4,12},{8,16},{12,20},{16,24},{20,28},{25,1},{... | collective-permute-start | bytes 786440 | tf_op jit(solution)/shard_map/ppermute | solution.py:23
  89.5 1.0 copy-start.4
  92.5 0.9 copy-start.2
  92.6 58.6 %all-gather.5.cloned.1.call-start = ((), (), s32[]{:S(2)}) async-start(), calls=%async_computation.4 | async-start | bytes 1310720 | tf_op jit(solution)/shard_map/all_gather | solution.py:226
  93.6 57.6 %copy-start.3 = (f32[2,128,512]{2,1,0:T(8,128)S(1)}, f32[2,128,512]{2,1,0:T(8,128)}, u32[]{:S(2)}) copy-start(f32[2,128,512]{2,1,0:T(8,128)} %param.11) | copy-start | bytes 1572868
  122.2 105.4 %reduce-scatter.5.cloned.1.call-start = ((), (), s32[]{:S(2)}) async-start(), calls=%async_computation.5 | async-start | bytes 1310720 | tf_op jit(solution)/shard_map/reduce_scatter | solution.py:251
  153.4 7.7 %collective-permute-start.6 = (f32[512,128]{1,0:T(8,128)S(1)}, f32[512,128]{1,0:T(8,128)S(1)}, u32[]{:S(2)}, u32[]{:S(2)}) collective-permute-start(f32[512,128]{1,0:T(8,128)S(1)} %fusion.2), channel_id=1, source_target_pairs={{4,0},{8,4},{12,8},{16,12},{20,16},{24,20},{28,24},{0,28},{5,1},{9... | collective-permute-start | bytes 786440 | tf_op jit(solution)/shard_map/ppermute | solution.py:23
  154.5 9.4 %collective-permute-start.7 = (f32[512,128]{1,0:T(8,128)S(1)}, f32[512,128]{1,0:T(8,128)S(1)}, u32[]{:S(2)}, u32[]{:S(2)}) collective-permute-start(f32[512,128]{1,0:T(8,128)S(1)} %fusion.2), channel_id=1, source_target_pairs={{8,0},{12,4},{16,8},{20,12},{24,16},{28,20},{0,24},{4,28},{9,1},{1... | collective-permute-start | bytes 786440 | tf_op jit(solution)/shard_map/ppermute | solution.py:23
  186.0 9.0 %collective-permute-start.8 = (f32[512,128]{1,0:T(8,128)S(1)}, f32[512,128]{1,0:T(8,128)S(1)}, u32[]{:S(2)}, u32[]{:S(2)}) collective-permute-start(f32[512,128]{1,0:T(8,128)S(1)} %bitcast.56), channel_id=1, source_target_pairs={{28,0},{0,4},{4,8},{8,12},{12,16},{16,20},{20,24},{24,28},{29,1},{... | collective-permute-start | bytes 786440 | tf_op jit(solution)/shard_map/ppermute | solution.py:23
  186.1 12.1 %collective-permute-start.9 = (f32[512,128]{1,0:T(8,128)S(1)}, f32[512,128]{1,0:T(8,128)S(1)}, u32[]{:S(2)}, u32[]{:S(2)}) collective-permute-start(f32[512,128]{1,0:T(8,128)S(1)} %bitcast.54), channel_id=1, source_target_pairs={{24,0},{28,4},{0,8},{4,12},{8,16},{12,20},{16,24},{20,28},{25,1},{... | collective-permute-start | bytes 786440 | tf_op jit(solution)/shard_map/ppermute | solution.py:23
  200.3 27.3 %copy-start.1 = (f32[128,512]{0,1:T(8,128)S(1)}, f32[128,512]{0,1:T(8,128)}, u32[]{:S(2)}) copy-start(f32[128,512]{0,1:T(8,128)} %multiply_add_fusion.1) | copy-start | bytes 786436
Sparse Core Ops, SparseCore 0:
  8.9 30.6 all-gather.2
  92.7 27.6 reduce-scatter.2
  122.3 28.8 all-gather.4
  200.4 27.0 reduce-scatter.4

commit v2 on v1

--- a/solution.py
+++ b/solution.py
@@ -198,6 +198,265 @@
     )(base, table, columns, rows, mapped, filters)
 
 
+HIGHEST = lax.Precision.HIGHEST
+MESH = pl.DeviceIdType.MESH
+
+
+def contract(left, right, left_dim, right_dim):
+    return lax.dot_general(
+        left,
+        right,
+        (((left_dim,), (right_dim,)), ((), ())),
+        precision=HIGHEST,
+        preferred_element_type=jnp.float32,
+    )
+
+
+def greet(reach):
+    space, chan = lax.axis_index("space"), lax.axis_index("chan")
+    spatial, groups = lax.axis_size("space"), lax.axis_size("chan")
+    barrier = pltpu.get_barrier_semaphore()
+    partners = [(space, lax.rem(chan + p, groups)) for p in range(1, groups)]
+    for offset in range(1, reach + 1):
+        partners.append((lax.rem(space + offset, spatial), chan))
+        partners.append((lax.rem(space + spatial - offset, spatial), chan))
+    for partner in partners:
+        pl.semaphore_signal(barrier, inc=1, device_id=partner, device_id_type=MESH)
+    pl.semaphore_wait(barrier, len(partners))
+    return space, chan, spatial, groups
+
+
+def send(source, target, sems, at, device):
+    copy = pltpu.make_async_remote_copy(
+        src_ref=source,
+        dst_ref=target,
+        send_sem=sems[0].at[at],
+        recv_sem=sems[1].at[at],
+        device_id=device,
+        device_id_type=MESH,
+    )
+    copy.start()
+    return copy
+
+
+def spread_block(out_ref, block, p, reach, blocks, place, sems):
+    space, chan, spatial, groups = place
+    copies = []
+    for offset in range(1, reach + 1):
+        copies.append(
+            send(
+                out_ref.at[block],
+                out_ref.at[offset * blocks + block],
+                sems,
+                (offset - 1, p),
+                (lax.rem(space + spatial - offset, spatial), chan),
+            )
+        )
+    return copies
+
+
+def gather_kernel(reach, feature_ref, weight_ref, out_ref, state_ref, landed, *sems):
+    place = greet(reach)
+    space, chan, spatial, groups = place
+    chan_sems, space_sems = sems[:2], sems[2:]
+    rows, _ = feature_ref.shape
+    extent = out_ref.shape[1]
+    arriving = {}
+    for q in range(groups):
+        for p in range(1, groups):
+            arriving[p, q] = send(
+                feature_ref.at[:, q * extent : (q + 1) * extent],
+                landed.at[p - 1, q],
+                chan_sems,
+                (p - 1, q),
+                (space, lax.rem(chan + p, groups)),
+            )
+    leaving = []
+    for q in range(groups):
+        total = 0.0
+        for p in range(groups):
+            if p > 0:
+                arriving[p, q].wait_recv()
+                part = landed[p - 1, q]
+            else:
+                part = feature_ref[:, q * extent : (q + 1) * extent]
+            source = lax.rem(chan + groups - p, groups)
+            columns = pl.ds(pl.multiple_of(source * rows, rows), rows)
+            total = total + contract(weight_ref[:, columns], part, 1, 0)
+        out_ref[q] = total.T
+        leaving += spread_block(out_ref, q, q, reach, groups, place, space_sems)
+    own = pl.ds(pl.multiple_of(chan * extent, extent), extent)
+    state_ref[chan] = feature_ref[:, own]
+    for p in range(1, groups):
+        state_ref[lax.rem(chan + groups - p, groups)] = landed[p - 1, chan]
+    for copy in arriving.values():
+        copy.wait_send()
+    for copy in leaving:
+        copy.wait()
+
+
+def mix_states(reach, collected_ref, state_ref, mix_ref, back, sums, heard, place, back_sems, sum_sems):
+    space, chan, spatial, groups = place
+    order = list(range(1, groups)) + [0]
+    copies, returning = [], {}
+    for p in order:
+        block = lax.rem(chan + p, groups)
+        for offset in range(1, reach + 1):
+            returning[offset, p] = send(
+                collected_ref.at[offset * groups + block],
+                back.at[offset - 1, p],
+                back_sems,
+                (offset - 1, p),
+                (lax.rem(space + offset, spatial), chan),
+            )
+    telling = {}
+    for p in order:
+        block = lax.rem(chan + p, groups)
+        total = collected_ref[block]
+        for offset in range(1, reach + 1):
+            returning[offset, p].wait_recv()
+            total = total + back[offset - 1, p]
+        sums[p] = total
+        if p > 0:
+            telling[p] = send(sums.at[p], heard.at[p - 1], sum_sems, (p - 1,), (space, block))
+    copies += list(returning.values()) + list(telling.values())
+
+    def weight(source):
+        held = mix_ref[:, source]
+        return held.reshape(held.shape[0] * held.shape[1], held.shape[2])
+
+    mixed = contract(weight(chan), sums[0], 1, 1)
+    for p in range(1, groups):
+        telling[p].wait_recv()
+        mixed = mixed + contract(weight(lax.rem(chan + groups - p, groups)), heard[p - 1], 1, 1)
+    old = state_ref[...]
+    mixed = mixed.reshape(old.shape)
+    return old + mixed / (1.0 + jnp.exp(-mixed)), copies
+
+
+def middle_kernel(
+    reach, collected_ref, state_ref, mix_ref, in_ref, out_ref, new_ref, back, sums, heard, ready, *sems
+):
+    place = greet(reach)
+    space, chan, spatial, groups = place
+    new_state, copies = mix_states(
+        reach, collected_ref, state_ref, mix_ref, back, sums, heard, place, sems[0:2], sems[2:4]
+    )
+    new_ref[...] = new_state
+    flat = new_state.reshape(new_state.shape[0] * new_state.shape[1], new_state.shape[2])
+    handing = {}
+    for p in list(range(1, groups)) + [0]:
+        target = lax.rem(chan + p, groups)
+        held = in_ref[:, target]
+        held = held.reshape(held.shape[0] * held.shape[1], held.shape[2])
+        mapped = contract(held, flat, 1, 0).T
+        if p > 0:
+            ready[p - 1] = mapped
+            handing[p] = send(ready.at[p - 1], out_ref.at[chan], sems[4:6], (p - 1,), (space, target))
+        else:
+            out_ref[chan] = mapped
+    leaving = spread_block(out_ref, chan, 0, reach, groups, place, sems[6:8])
+    for p in range(1, groups):
+        handing[p].wait_recv()
+        block = lax.rem(chan + groups - p, groups)
+        leaving += spread_block(out_ref, block, p, reach, groups, place, sems[6:8])
+    for copy in copies + list(handing.values()):
+        copy.wait_send()
+    for copy in leaving:
+        copy.wait()
+
+
+def last_kernel(reach, collected_ref, state_ref, mix_ref, out_ref, back, sums, heard, ready, *sems):
+    place = greet(reach)
+    space, chan, spatial, groups = place
+    new_state, copies = mix_states(
+        reach, collected_ref, state_ref, mix_ref, back, sums, heard, place, sems[0:2], sems[2:4]
+    )
+    ready[...] = new_state
+    extent = ready.shape[2]
+    own = pl.ds(pl.multiple_of(chan * extent, extent), extent)
+    handing = {}
+    for p in range(1, groups):
+        target = lax.rem(chan + p, groups)
+        handing[p] = send(ready.at[target], out_ref.at[:, own], sems[4:6], (p - 1,), (space, target))
+    out_ref[:, own] = ready[chan]
+    for p in range(1, groups):
+        handing[p].wait_recv()
+    for copy in copies + list(handing.values()):
+        copy.wait_send()
+
+
+def remote_call(kernel, outs, scratch, pairs, collective, *operands):
+    vmem = pl.BlockSpec(memory_space=pltpu.VMEM)
+    sems = [pltpu.SemaphoreType.DMA(shape) for shape in pairs for _ in range(2)]
+    return pl.pallas_call(
+        kernel,
+        out_shape=[jax.ShapeDtypeStruct(shape, jnp.float32) for shape in outs],
+        in_specs=[vmem] * len(operands),
+        out_specs=[vmem] * len(outs),
+        scratch_shapes=[pltpu.VMEM(shape, jnp.float32) for shape in scratch] + sems,
+        compiler_params=pltpu.CompilerParams(
+            collective_id=collective, has_side_effects=True, vmem_limit_bytes=40 * 1024 * 1024
+        ),
+    )(*operands)
+
+
+def all_pieces(local, own_index, spatial):
+    part = local.shape[0] // spatial
+    share = lax.dynamic_slice_in_dim(local, own_index * part, part, 0)
+    gathered = lax.all_gather(share, ("space", "chan"), axis=0, tiled=False)
+    return gathered.reshape(spatial, lax.axis_size("chan"), part, local.shape[1])
+
+
+def exchanged_layers(features, mix_weight, in_weight, own_index, reach, blocks, block_len, pairs_of):
+    spatial, groups = lax.axis_size("space"), lax.axis_size("chan")
+    channels = features.shape[0]
+    slots = (reach + 1) * blocks
+    mix_full = [all_pieces(mix_weight[0], own_index, spatial)]
+    in_full = [None]
+    for layer in range(1, LAYERS):
+        in_full.append(all_pieces(in_weight[layer], own_index, spatial))
+        mix_full.append(all_pieces(mix_weight[layer], own_index, spatial))
+    blocked = (slots, block_len, channels)
+    held = (groups, channels, block_len)
+    square = (block_len, channels)
+    mapped, state = remote_call(
+        functools.partial(gather_kernel, reach),
+        [blocked, held],
+        [(groups - 1, groups, channels, block_len)],
+        [(groups - 1, groups), (reach, groups)],
+        0,
+        features,
+        in_weight[0],
+    )
+    scratch = [(reach, groups, *square), (groups, *square), (groups - 1, *square)]
+    for layer in range(LAYERS - 1):
+        collected = pairs_of(mapped, layer)
+        mapped, state = remote_call(
+            functools.partial(middle_kernel, reach),
+            [blocked, held],
+            scratch + [(groups - 1, *square)],
+            [(reach, groups), (groups - 1,), (groups - 1,), (reach, groups)],
+            1,
+            collected,
+            state,
+            mix_full[layer],
+            in_full[layer + 1],
+        )
+    collected = pairs_of(mapped, LAYERS - 1)
+    (updated,) = remote_call(
+        functools.partial(last_kernel, reach),
+        [features.shape],
+        scratch + [held],
+        [(reach, groups), (groups - 1,), (groups - 1,)],
+        2,
+        collected,
+        state,
+        mix_full[LAYERS - 1],
+    )
+    return updated
+
+
 def shards(positions, features, block_counts, pair_table, in_weight, filter_weight, mix_weight):
     spatial = lax.axis_size("space")
     reach_dev = spatial // 4
@@ -221,6 +480,24 @@
     )
     columns = rows.transpose(0, 2, 1)
     base = jnp.stack([own_index, jnp.int32(spatial)]).astype(jnp.int32)
+    groups = lax.axis_size("chan")
+
+    def pairs_of(mapped_blocks, layer):
+        return pair_messages(
+            base, pair_table, columns, rows, mapped_blocks, filter_weight[layer], blocks
+        )
+
+    whole_tiles = (
+        local_chan % 128 == 0
+        and block_len % 128 == 0
+        and blocks == groups
+        and spatial > 2 * reach_dev
+        and local_chan % (8 * spatial) == 0
+    )
+    if whole_tiles:
+        return exchanged_layers(
+            features, mix_weight, in_weight, own_index, reach_dev, blocks, block_len, pairs_of
+        )
     state = features
     for layer in range(LAYERS):
         full_state = lax.all_gather(state, "chan", axis=0, tiled=True)
@@ -235,9 +512,7 @@
         for offset in range(1, reach_dev + 1):
             neighbours.append(shifted(mapped, "space", -offset))
         mapped_blocks = jnp.concatenate(neighbours, axis=0).reshape(slot_total, block_len, local_chan)
-        collected = pair_messages(
-            base, pair_table, columns, rows, mapped_blocks, filter_weight[layer], blocks
-        ).reshape(reach_dev + 1, atoms_dev, local_chan)
+        collected = pairs_of(mapped_blocks, layer).reshape(reach_dev + 1, atoms_dev, local_chan)
         received = collected[0]
         for offset in range(1, reach_dev + 1):
             received = received + shifted(collected[offset], "space", offset)

time: 237 us -> 213 us (0.90)
  Pallas kernels: 44 us -> 126 us
  waiting for transfers between devices: 142 us -> 61.3 us
  starting transfers between devices: 19.4 us -> 4.04 us
  matrix products: 9.27 us -> 0 us
  local copies, waits for them, and re-layouts: 4.46 us -> 8.44 us
  other arithmetic: 3.31 us -> 0.37 us
    pallas_call x0 -> x3, Pallas kernels: none -> 84.7 us  [remote_call(): pl.pallas_call(kernel, out_shape=[jax.ShapeDtypeStruct(shape, jnp.float32...]
    reduce_scatter x2 -> x0, waiting for transfers between devices: 54.1 us -> none  [shards(): own_mixed = lax.psum_scatter(mixed, 'chan', scatter_dimension=0, tiled=True)]
    ppermute x10 -> x2, waiting for transfers between devices: 31 us -> 0.01 us  [shifted(): return lax.ppermute(block, axis, route)]
    ppermute x10 -> x2, starting transfers between devices: 19.3 us -> 3.95 us  [shifted(): return lax.ppermute(block, axis, route)]
    dot_general x4 -> x0, matrix products: 9.27 us -> none  [the longest x2 5.27 us: shards(): lax.dot_general(full_state, in_weight[layer], (((0,), (1,)), ((), ())), p...]
    all_gather x2 -> x3, waiting for transfers between devices: 56.4 us -> 61.2 us  [all_pieces(): gathered = lax.all_gather(share, ('space', 'chan'), axis=0, tiled=False)]
    pallas_call x2, Pallas kernels: 44 us -> 40.8 us  [pair_messages(): pl.pallas_call(functools.partial(pair_kernel, blocks), out_shape=jax.Shap...]
    add x4 -> x0, other arithmetic: 2.83 us -> none  [the longest x2 2.76 us: shards(): state = state + jax.nn.silu(own_mixed)]
  transfers between devices with their start and end apart: 14 -> 5, of which waited for: 12 -> 3; matrix products, arithmetic and copies ran while one was open for 2% -> 1% of each run, Pallas kernels for 0% -> 48%
where the time goes in v2:
time: 213 us
  Pallas kernels  126 us (59%)
  waiting for transfers between devices  61.3 us (29%)
  between operations  13.2 us (6%)
  local copies, waits for them, and re-layouts  8.44 us (4%)
  starting transfers between devices  4.04 us (2%)
    pallas_call x3, Pallas kernels, remote_call(): pl.pallas_call(kernel, out_shape=[jax.ShapeDtypeStruct(shape, jnp.float32...  84.7 us
    all_gather x3, waiting for transfers between devices, all_pieces(): gathered = lax.all_gather(share, ('space', 'chan'), axis=0, tiled=False)  61.2 us
    pallas_call x2, Pallas kernels, pair_messages(): pl.pallas_call(functools.partial(pair_kernel, blocks), out_shape=jax.Shap...  40.8 us
    unnamed x19, local copies, waits for them, and re-layouts  5.09 us
  transfers between devices with their start and end apart: 5, of which 3 were waited for; matrix products, arithmetic and copies ran while one was open for 1% of the time, Pallas kernels for 48%

profile of v2, /device:TPU:0, one launch (start us, length us, event | category | flops | bytes accessed | tf_op | source)
XLA Modules:
  0.0 212.9 jit_solution(9994450429283857388)
XLA Ops:
  6.5 1.1 fusion.2
  7.7 0.6 constant_dynamic-slice_fusion.2
  8.3 0.0 all-gather.4.cloned.1.call-update
  8.3 0.0 all-gather.6.cloned.1.call-start
  8.4 0.0 copy-start.7
  8.5 0.6 constant_dynamic-slice_fusion.1
  9.1 0.0 all-gather.6.cloned.1.call-update
  9.1 0.0 all-gather.8.cloned.1.call-start
  9.2 0.6 constant_dynamic-slice_fusion
  9.8 0.1 all-gather.8.cloned.1.call-update
  9.9 0.1 pad.8.clone
  9.9 0.1 fusion
  10.0 0.1 maximum_maximum_fusion
  10.1 3.3 %collective-permute-start = (f32[8,512]{1,0:T(8,128)S(1)}, f32[8,512]{1,0:T(8,128)S(1)}, u32[]{:S(2)}, u32[]{:S(2)}) collective-permute-start(f32[8,512]{1,0:T(8,128)S(1)} %maximum_maximum_fusion), channel_id=1, source_target_pairs={{4,0},{8,4},{12,8},{16,12},{20,16},{24,20},{28,24},{0,28},{5,1},{9... | collective-permute-start | bytes 49160 | tf_op jit(solution)/shard_map/ppermute | solution.py:23
  13.4 0.6 collective-permute-start.1
  14.0 0.1 compare_convert_fusion
  14.1 0.1 maximum_bitcast_fusion
  14.2 0.1 pad_add_fusion.base_ref
  14.3 32.2 %shard_map.73 = (f32[12,128,128]{2,1,0:T(8,128)S(1)}, f32[4,128,128]{2,1,0:T(8,128)S(1)}) custom-call(f32[128,512]{1,0:T(8,128)S(1)} %copy-done.3, f32[128,512]{1,0:T(8,128)S(1)} %get-tuple-element.16.weight_ref), custom_call_target="tpu_custom_call" | custom-call | tf_op jit(solution)/shard_map/pallas_call | solution.py:392
  46.5 0.3 copy.11.columns_ref
  46.8 0.7 copy-done.4
  47.5 20.4 %shard_map.74.collected_ref = f32[12,128,128]{2,1,0:T(8,128)S(1)} custom-call(s32[2]{0:T(128)S(1)} %pad_add_fusion.base_ref, s32[3,64]{1,0:T(4,128)S(1)} %copy-done.4, f32[12,128,8]{2,1,0:T(8,128)S(1)} %copy.11.columns_ref, f32[12,8,128]{2,1,0:T(8,128)S(1)} %get-tuple-element.17.rows_ref, f32[12,128,128]{2,1,0:T(8,128)S(1)} %get-tuple-element.9.mapped_ref, ...), custom_call_target="tpu_custom_call" | custom-call | tf_op jit(solution)/shard_map/pallas_call | solution.py:182
  67.9 1.3 all-gather.4.cloned.1.call-done
  69.2 55.7 %all-gather.6.cloned.1.call-done = f32[32,16,512]{2,1,0:T(8,128)} async-done(((f32[1,16,512]{2,1,0:T(8,128)}), f32[32,16,512]{2,1,0:T(8,128)}) %all-gather.6.cloned.1.call-update) | async-done | bytes 1048592 | tf_op jit(solution)/shard_map/all_gather | solution.py:407
  125.0 1.2 copy-done
  126.2 1.2 copy-done.1
  127.4 30.1 %shard_map.75 = (f32[12,128,128]{2,1,0:T(8,128)S(1)}, f32[4,128,128]{2,1,0:T(8,128)S(1)}) custom-call(f32[12,128,128]{2,1,0:T(8,128)S(1)} %shard_map.74.collected_ref, f32[4,128,128]{2,1,0:T(8,128)S(1)} %get-tuple-element.10.state_ref, f32[8,4,64,128]{3,2,1,0:T(8,128)S(1)} %bitcast.22, f32[8,4,16,512]{3,2,1,0:T(8,128)S(1)} %bitcast.23), custom_call_target="tpu_custom_call" | custom-call | tf_op jit(solution)/shard_map/pallas_call | solution.py:392
  157.6 20.4 %shard_map.76.collected_ref = f32[12,128,128]{2,1,0:T(8,128)S(1)} custom-call(s32[2]{0:T(128)S(1)} %pad_add_fusion.base_ref, s32[3,64]{1,0:T(4,128)S(1)} %copy-done.4, f32[12,128,8]{2,1,0:T(8,128)S(1)} %copy.11.columns_ref, f32[12,8,128]{2,1,0:T(8,128)S(1)} %get-tuple-element.17.rows_ref, f32[12,128,128]{2,1,0:T(8,128)S(1)} %get-tuple-element.11.mapped_ref, ...), custom_call_target="tpu_custom_call" | custom-call | tf_op jit(solution)/shard_map/pallas_call | solution.py:182
  178.0 4.1 %all-gather.8.cloned.1.call-done = f32[32,64,128]{2,1,0:T(8,128)} async-done(((f32[1,64,128]{2,1,0:T(8,128)}), f32[32,64,128]{2,1,0:T(8,128)}) %all-gather.8.cloned.1.call-update) | async-done | bytes 1048592 | tf_op jit(solution)/shard_map/all_gather | solution.py:407
  182.1 1.2 copy-done.2
  183.3 22.3 %shard_map.77 = f32[128,512]{1,0:T(8,128)S(1)} custom-call(f32[12,128,128]{2,1,0:T(8,128)S(1)} %shard_map.76.collected_ref, f32[4,128,128]{2,1,0:T(8,128)S(1)} %get-tuple-element.12.state_ref, f32[8,4,64,128]{3,2,1,0:T(8,128)S(1)} %bitcast.24), custom_call_target="tpu_custom_call" | custom-call | tf_op jit(solution)/shard_map/pallas_call | solution.py:392
  205.6 0.7 copy.13
  (20 shorter events, 0.1 us)
Async XLA Ops:
  6.5 62.7 %all-gather.4.cloned.1.call-start = ((), (), s32[]{:S(2)}) async-start(), calls=%async_computation | async-start | bytes 1081344 | tf_op jit(solution)/shard_map/all_gather | solution.py:407
  6.5 1.8 copy-start.5
  8.3 116.7 %all-gather.6.cloned.1.call-start = ((), (), s32[]{:S(2)}) async-start(), calls=%async_computation.1 | async-start | bytes 1081344 | tf_op jit(solution)/shard_map/all_gather | solution.py:407
  8.4 1.6 copy-start.8
  8.4 1.6 copy-start.6
  8.4 5.7 %copy-start.7 = (f32[2,8,128]{2,1,0:T(8,128)S(1)}, f32[2,8,128]{2,1,0:T(8,128)}, u32[]{:S(2)}) copy-start(f32[2,8,128]{2,1,0:T(8,128)} %param.12) | copy-start | bytes 24580
  8.5 5.8 %copy-start.3 = (f32[128,512]{1,0:T(8,128)S(1)}, f32[128,512]{1,0:T(8,128)}, u32[]{:S(2)}) copy-start(f32[128,512]{1,0:T(8,128)} %feature_ref.1) | copy-start | bytes 786436
  9.1 172.9 %all-gather.8.cloned.1.call-start = ((), (), s32[]{:S(2)}) async-start(), calls=%async_computation.2 | async-start | bytes 1081344 | tf_op jit(solution)/shard_map/all_gather | solution.py:407
  10.1 36.4 %collective-permute-start = (f32[8,512]{1,0:T(8,128)S(1)}, f32[8,512]{1,0:T(8,128)S(1)}, u32[]{:S(2)}, u32[]{:S(2)}) collective-permute-start(f32[8,512]{1,0:T(8,128)S(1)} %maximum_maximum_fusion), channel_id=1, source_target_pairs={{4,0},{8,4},{12,8},{16,12},{20,16},{24,20},{28,24},{0,28},{5,1},{9... | collective-permute-start | bytes 49160 | tf_op jit(solution)/shard_map/ppermute | solution.py:23
  13.4 33.1 %collective-permute-start.1 = (f32[8,512]{1,0:T(8,128)S(1)}, f32[8,512]{1,0:T(8,128)S(1)}, u32[]{:S(2)}, u32[]{:S(2)}) collective-permute-start(f32[8,512]{1,0:T(8,128)S(1)} %maximum_maximum_fusion), channel_id=1, source_target_pairs={{8,0},{12,4},{16,8},{20,12},{24,16},{28,20},{0,24},{4,28},{9,1},{1... | collective-permute-start | bytes 49160 | tf_op jit(solution)/shard_map/ppermute | solution.py:23
  46.8 0.7 copy-start.4
  125.0 1.2 copy-start
  126.2 1.2 copy-start.1
  182.1 1.2 copy-start.2
Sparse Core Ops, SparseCore 0:
  10.3 58.8 all-gather.3
  72.2 52.7 all-gather.5
  128.0 54.0 all-gather.7

commit v3 on v2

--- a/solution.py
+++ b/solution.py
@@ -212,14 +212,16 @@
     )
 
 
-def greet(reach):
+def greet(reach, stride=None):
     space, chan = lax.axis_index("space"), lax.axis_index("chan")
     spatial, groups = lax.axis_size("space"), lax.axis_size("chan")
     barrier = pltpu.get_barrier_semaphore()
     partners = [(space, lax.rem(chan + p, groups)) for p in range(1, groups)]
-    for offset in range(1, reach + 1):
+    offsets = set(range(1, reach + 1)) | {spatial - offset for offset in range(1, reach + 1)}
+    if stride is not None:
+        offsets |= set(range(stride, spatial, stride))
+    for offset in sorted(offsets):
         partners.append((lax.rem(space + offset, spatial), chan))
-        partners.append((lax.rem(space + spatial - offset, spatial), chan))
     for partner in partners:
         pl.semaphore_signal(barrier, inc=1, device_id=partner, device_id_type=MESH)
     pl.semaphore_wait(barrier, len(partners))
@@ -255,14 +257,65 @@
     return copies
 
 
-def gather_kernel(reach, feature_ref, weight_ref, out_ref, state_ref, landed, *sems):
-    place = greet(reach)
+def gather_kernel(
+    reach,
+    geometry_ref,
+    feature_ref,
+    weight_ref,
+    mix_ref,
+    out_ref,
+    state_ref,
+    rows_ref,
+    columns_ref,
+    all_mix_ref,
+    all_in_ref,
+    landed,
+    *sems,
+):
+    place = greet(reach, 2)
     space, chan, spatial, groups = place
-    chan_sems, space_sems = sems[:2], sems[2:]
+    chan_sems, space_sems, near_sems, piece_sems, far_sems, pair_sems = (
+        sems[2 * i : 2 * i + 2] for i in range(6)
+    )
     rows, _ = feature_ref.shape
     extent = out_ref.shape[1]
+    blocks = geometry_ref.shape[0]
+
+    shares = []
+    for source, target in ((mix_ref, all_mix_ref), (weight_ref, all_in_ref)):
+        part = target.shape[-2]
+        mine = pl.ds(pl.multiple_of(space * part, part), part)
+        if target is all_in_ref:
+            held = source.at[pl.ds(1, LAYERS - 1), mine]
+        else:
+            held = source.at[:, mine]
+        shares.append((held, target))
+    pieces, leaving = [], []
+    for p in range(1, groups):
+        for kind, (held, target) in enumerate(shares):
+            pieces.append(
+                send(
+                    held,
+                    target.at[space, chan],
+                    piece_sems,
+                    (kind, p - 1),
+                    (space, lax.rem(chan + p, groups)),
+                )
+            )
+    rows_ref[:blocks] = geometry_ref[...]
+    for offset in range(1, reach + 1):
+        leaving.append(
+            send(
+                geometry_ref,
+                rows_ref.at[pl.ds(offset * blocks, blocks)],
+                near_sems,
+                (offset - 1,),
+                (lax.rem(space + spatial - offset, spatial), chan),
+            )
+        )
     arriving = {}
-    for q in range(groups):
+
+    def tell(q):
         for p in range(1, groups):
             arriving[p, q] = send(
                 feature_ref.at[:, q * extent : (q + 1) * extent],
@@ -271,7 +324,32 @@
                 (p - 1, q),
                 (space, lax.rem(chan + p, groups)),
             )
-    leaving = []
+
+    tell(0)
+    for held, target in shares:
+        target[space, chan] = held[...]
+    for copy in pieces:
+        copy.wait_recv()
+    far, paired = [], []
+    partner = (space + 1 - 2 * lax.rem(space, 2), chan)
+    for kind, (_, target) in enumerate(shares):
+        for hop in range(1, spatial // 2):
+            far.append(
+                (
+                    send(
+                        target.at[space],
+                        target.at[space],
+                        far_sems,
+                        (kind, hop - 1),
+                        (lax.rem(space + 2 * hop, spatial), chan),
+                    ),
+                    kind,
+                    hop,
+                )
+            )
+        paired.append(send(target.at[space], target.at[space], pair_sems, (kind, 0), partner))
+    for q in range(1, groups):
+        tell(q)
     for q in range(groups):
         total = 0.0
         for p in range(groups):
@@ -282,20 +360,27 @@
                 part = feature_ref[:, q * extent : (q + 1) * extent]
             source = lax.rem(chan + groups - p, groups)
             columns = pl.ds(pl.multiple_of(source * rows, rows), rows)
-            total = total + contract(weight_ref[:, columns], part, 1, 0)
+            total = total + contract(weight_ref[0, :, columns], part, 1, 0)
         out_ref[q] = total.T
         leaving += spread_block(out_ref, q, q, reach, groups, place, space_sems)
     own = pl.ds(pl.multiple_of(chan * extent, extent), extent)
     state_ref[chan] = feature_ref[:, own]
     for p in range(1, groups):
         state_ref[lax.rem(chan + groups - p, groups)] = landed[p - 1, chan]
-    for copy in arriving.values():
+    for copy, kind, hop in far:
+        copy.wait_recv()
+        source = lax.rem(space + spatial - 2 * hop, spatial)
+        target = shares[kind][1]
+        paired.append(send(target.at[source], target.at[source], pair_sems, (kind, hop), partner))
+    for copy in leaving + paired:
+        copy.wait()
+    for at in range(rows_ref.shape[0]):
+        columns_ref[at] = rows_ref[at].T
+    for copy in list(arriving.values()) + pieces + [copy for copy, _, _ in far]:
         copy.wait_send()
-    for copy in leaving:
-        copy.wait()
-
-
-def mix_states(reach, collected_ref, state_ref, mix_ref, back, sums, heard, place, back_sems, sum_sems):
+
+
+def mix_states(reach, layer, collected_ref, state_ref, mix_ref, back, sums, heard, place, back_sems, sum_sems):
     space, chan, spatial, groups = place
     order = list(range(1, groups)) + [0]
     copies, returning = [], {}
@@ -322,7 +407,7 @@
     copies += list(returning.values()) + list(telling.values())
 
     def weight(source):
-        held = mix_ref[:, source]
+        held = mix_ref[:, source, layer]
         return held.reshape(held.shape[0] * held.shape[1], held.shape[2])
 
     mixed = contract(weight(chan), sums[0], 1, 1)
@@ -335,19 +420,31 @@
 
 
 def middle_kernel(
-    reach, collected_ref, state_ref, mix_ref, in_ref, out_ref, new_ref, back, sums, heard, ready, *sems
+    reach,
+    layer,
+    collected_ref,
+    state_ref,
+    mix_ref,
+    in_ref,
+    out_ref,
+    new_ref,
+    back,
+    sums,
+    heard,
+    ready,
+    *sems,
 ):
     place = greet(reach)
     space, chan, spatial, groups = place
     new_state, copies = mix_states(
-        reach, collected_ref, state_ref, mix_ref, back, sums, heard, place, sems[0:2], sems[2:4]
+        reach, layer, collected_ref, state_ref, mix_ref, back, sums, heard, place, sems[0:2], sems[2:4]
     )
     new_ref[...] = new_state
     flat = new_state.reshape(new_state.shape[0] * new_state.shape[1], new_state.shape[2])
     handing = {}
     for p in list(range(1, groups)) + [0]:
         target = lax.rem(chan + p, groups)
-        held = in_ref[:, target]
+        held = in_ref[:, target, layer]
         held = held.reshape(held.shape[0] * held.shape[1], held.shape[2])
         mapped = contract(held, flat, 1, 0).T
         if p > 0:
@@ -366,11 +463,11 @@
         copy.wait()
 
 
-def last_kernel(reach, collected_ref, state_ref, mix_ref, out_ref, back, sums, heard, ready, *sems):
+def last_kernel(reach, layer, collected_ref, state_ref, mix_ref, out_ref, back, sums, heard, ready, *sems):
     place = greet(reach)
     space, chan, spatial, groups = place
     new_state, copies = mix_states(
-        reach, collected_ref, state_ref, mix_ref, back, sums, heard, place, sems[0:2], sems[2:4]
+        reach, layer, collected_ref, state_ref, mix_ref, back, sums, heard, place, sems[0:2], sems[2:4]
     )
     ready[...] = new_state
     extent = ready.shape[2]
@@ -401,58 +498,66 @@
     )(*operands)
 
 
-def all_pieces(local, own_index, spatial):
-    part = local.shape[0] // spatial
-    share = lax.dynamic_slice_in_dim(local, own_index * part, part, 0)
-    gathered = lax.all_gather(share, ("space", "chan"), axis=0, tiled=False)
-    return gathered.reshape(spatial, lax.axis_size("chan"), part, local.shape[1])
-
-
-def exchanged_layers(features, mix_weight, in_weight, own_index, reach, blocks, block_len, pairs_of):
+def exchanged_layers(geometry, features, in_weight, mix_weight, reach, pairs_of):
     spatial, groups = lax.axis_size("space"), lax.axis_size("chan")
+    blocks, _, block_len = geometry.shape
     channels = features.shape[0]
     slots = (reach + 1) * blocks
-    mix_full = [all_pieces(mix_weight[0], own_index, spatial)]
-    in_full = [None]
-    for layer in range(1, LAYERS):
-        in_full.append(all_pieces(in_weight[layer], own_index, spatial))
-        mix_full.append(all_pieces(mix_weight[layer], own_index, spatial))
     blocked = (slots, block_len, channels)
     held = (groups, channels, block_len)
     square = (block_len, channels)
-    mapped, state = remote_call(
+    hops = spatial // 2
+    mix_part = mix_weight.shape[1] // spatial
+    in_part = in_weight.shape[1] // spatial
+    mapped, state, rows, columns, all_mix, all_in = remote_call(
         functools.partial(gather_kernel, reach),
-        [blocked, held],
+        [
+            blocked,
+            held,
+            (slots, 8, block_len),
+            (slots, block_len, 8),
+            (spatial, groups, LAYERS, mix_part, mix_weight.shape[2]),
+            (spatial, groups, LAYERS - 1, in_part, in_weight.shape[2]),
+        ],
         [(groups - 1, groups, channels, block_len)],
-        [(groups - 1, groups), (reach, groups)],
+        [
+            (groups - 1, groups),
+            (reach, groups),
+            (reach,),
+            (2, groups - 1),
+            (2, hops - 1),
+            (2, hops),
+        ],
         0,
+        geometry,
         features,
-        in_weight[0],
+        in_weight,
+        mix_weight,
     )
     scratch = [(reach, groups, *square), (groups, *square), (groups - 1, *square)]
     for layer in range(LAYERS - 1):
-        collected = pairs_of(mapped, layer)
+        collected = pairs_of(columns, rows, mapped, layer)
         mapped, state = remote_call(
-            functools.partial(middle_kernel, reach),
+            functools.partial(middle_kernel, reach, layer),
             [blocked, held],
             scratch + [(groups - 1, *square)],
             [(reach, groups), (groups - 1,), (groups - 1,), (reach, groups)],
             1,
             collected,
             state,
-            mix_full[layer],
-            in_full[layer + 1],
+            all_mix,
+            all_in,
         )
-    collected = pairs_of(mapped, LAYERS - 1)
+    collected = pairs_of(columns, rows, mapped, LAYERS - 1)
     (updated,) = remote_call(
-        functools.partial(last_kernel, reach),
+        functools.partial(last_kernel, reach, LAYERS - 1),
         [features.shape],
         scratch + [held],
         [(reach, groups), (groups - 1,), (groups - 1,)],
         2,
         collected,
         state,
-        mix_full[LAYERS - 1],
+        all_mix,
     )
     return updated
 
@@ -472,17 +577,11 @@
         .reshape(1, atoms_dev)
     )
     geometry = jnp.concatenate([positions, valid, jnp.zeros((4, atoms_dev), jnp.float32)], axis=0)
-    fetched = [geometry]
-    for offset in range(1, reach_dev + 1):
-        fetched.append(shifted(geometry, "space", -offset))
-    rows = jnp.concatenate(
-        [part.reshape(8, blocks, block_len).transpose(1, 0, 2) for part in fetched], axis=0
-    )
-    columns = rows.transpose(0, 2, 1)
+    geometry = geometry.reshape(8, blocks, block_len).transpose(1, 0, 2)
     base = jnp.stack([own_index, jnp.int32(spatial)]).astype(jnp.int32)
     groups = lax.axis_size("chan")
 
-    def pairs_of(mapped_blocks, layer):
+    def pairs_of(columns, rows, mapped_blocks, layer):
         return pair_messages(
             base, pair_table, columns, rows, mapped_blocks, filter_weight[layer], blocks
         )
@@ -492,12 +591,16 @@
         and block_len % 128 == 0
         and blocks == groups
         and spatial > 2 * reach_dev
+        and spatial % 2 == 0
         and local_chan % (8 * spatial) == 0
     )
     if whole_tiles:
-        return exchanged_layers(
-            features, mix_weight, in_weight, own_index, reach_dev, blocks, block_len, pairs_of
-        )
+        return exchanged_layers(geometry, features, in_weight, mix_weight, reach_dev, pairs_of)
+    fetched = [geometry]
+    for offset in range(1, reach_dev + 1):
+        fetched.append(shifted(geometry, "space", -offset))
+    rows = jnp.concatenate(fetched, axis=0)
+    columns = rows.transpose(0, 2, 1)
     state = features
     for layer in range(LAYERS):
         full_state = lax.all_gather(state, "chan", axis=0, tiled=True)
@@ -512,7 +615,7 @@
         for offset in range(1, reach_dev + 1):
             neighbours.append(shifted(mapped, "space", -offset))
         mapped_blocks = jnp.concatenate(neighbours, axis=0).reshape(slot_total, block_len, local_chan)
-        collected = pairs_of(mapped_blocks, layer).reshape(reach_dev + 1, atoms_dev, local_chan)
+        collected = pairs_of(columns, rows, mapped_blocks, layer).reshape(reach_dev + 1, atoms_dev, local_chan)
         received = collected[0]
         for offset in range(1, reach_dev + 1):
             received = received + shifted(collected[offset], "space", offset)

time: 213 us -> 155 us (0.73)
  waiting for transfers between devices: 61.3 us -> 0 us
  Pallas kernels: 126 us -> 148 us
  between operations: 13.2 us -> 0.07 us
  starting transfers between devices: 4.04 us -> 0 us
  local copies, waits for them, and re-layouts: 8.44 us -> 5.2 us
    all_gather x3 -> x0, waiting for transfers between devices: 61.2 us -> none  [all_pieces(): gathered = lax.all_gather(share, ('space', 'chan'), axis=0, tiled=False)]
    pallas_call x3, Pallas kernels: 84.7 us -> 121 us  [remote_call(): pl.pallas_call(kernel, out_shape=[jax.ShapeDtypeStruct(shape, jnp.float32...]
    pallas_call x2, Pallas kernels: 40.8 us -> 26.2 us  [pair_messages(): pl.pallas_call(functools.partial(pair_kernel, blocks), out_shape=jax.Shap...]
    ppermute x2 -> x0, starting transfers between devices: 3.95 us -> none  [shifted(): return lax.ppermute(block, axis, route)]
    unnamed x19 -> x11, local copies, waits for them, and re-layouts: 5.09 us -> 4.42 us
  transfers between devices with their start and end apart: 5 -> 0, of which waited for: 3 -> 0; matrix products, arithmetic and copies ran while one was open for 1% -> 0% of each run, Pallas kernels for 48% -> 0%
where the time goes in v3:
time: 155 us; the launch traced here: 154 us
  Pallas kernels  148 us (95%)
  local copies, waits for them, and re-layouts  5.2 us (3%)
  other arithmetic  1.57 us (1%)
    pallas_call x3, Pallas kernels, remote_call(): pl.pallas_call(kernel, out_shape=[jax.ShapeDtypeStruct(shape, jnp.float32...  121 us
    pallas_call x2, Pallas kernels, pair_messages(): pl.pallas_call(functools.partial(pair_kernel, blocks), out_shape=jax.Shap...  26.2 us
    unnamed x11, local copies, waits for them, and re-layouts  4.42 us

profile of v3, /device:TPU:0, one launch (start us, length us, event | category | flops | bytes accessed | tf_op | source)
XLA Modules:
  0.0 154.5 jit_solution(16448743128416709394)
XLA Ops:
  0.0 0.1 pad_add_fusion.base_ref
  0.1 0.1 pad.2.clone
  0.2 0.7 compare_convert_fusion
  0.9 0.7 slice_bitcast_fusion
  1.6 0.8 maximum_bitcast_fusion.geometry_ref
  2.4 0.0 copy-start
  2.4 1.0 copy-done
  3.4 0.0 copy-start.1
  3.4 1.0 copy-done.1
  4.4 0.0 copy-start.2
  4.4 0.9 copy-done.2
  5.4 42.6 %shard_map.73 = (f32[12,128,128]{2,1,0:T(8,128)S(1)}, f32[4,128,128]{2,1,0:T(8,128)S(1)}, f32[12,8,128]{2,1,0:T(8,128)S(1)}, f32[12,128,8]{2,1,0:T(8,128)S(1)}, ...) custom-call(f32[4,8,128]{2,1,0:T(8,128)S(1)} %maximum_bitcast_fusion.geometry_ref, ...), custom_call_target="tpu_custom_call" | custom-call | tf_op jit(solution)/shard_map/pallas_call | solution.py:489
  48.0 0.0 copy-start.3
  48.0 0.7 copy-done.3
  48.7 13.1 %shard_map.74.collected_ref = f32[12,128,128]{2,1,0:T(8,128)S(1)} custom-call(s32[2]{0:T(128)S(1)} %pad_add_fusion.base_ref, s32[3,64]{1,0:T(4,128)S(1)} %copy-done.3, f32[12,128,8]{2,1,0:T(8,128)S(1)} %get-tuple-element.13.columns_ref, f32[12,8,128]{2,1,0:T(8,128)S(1)} %get-tuple-element.14.rows_ref, f32[12,128,128]{2,1,0:T(8,128)S(1)} %get-tuple-element.15.mapped_ref, ...), custom_call_target="tpu_custom_call" | custom-call | tf_op jit(solution)/shard_map/pallas_call | solution.py:182
  61.8 0.0 copy-start.4
  61.8 44.3 %shard_map.75 = (f32[12,128,128]{2,1,0:T(8,128)S(1)}, f32[4,128,128]{2,1,0:T(8,128)S(1)}) custom-call(f32[12,128,128]{2,1,0:T(8,128)S(1)} %shard_map.74.collected_ref, f32[4,128,128]{2,1,0:T(8,128)S(1)} %get-tuple-element.16.state_ref, f32[8,4,2,64,128]{4,3,2,1,0:T(8,128)S(1)} %get-tuple-element.17.mix_ref, f32[8,4,1,16,512]{4,3,2,1,0:T(8,128)S(1)} %get-tuple-element.18.in_ref), custom_call_target="tpu_custom_call" | custom-call | tf_op jit(solution)/shard_map/pallas_call | solution.py:489
  106.1 0.0 copy-done.4
  106.2 13.1 %shard_map.76.collected_ref = f32[12,128,128]{2,1,0:T(8,128)S(1)} custom-call(s32[2]{0:T(128)S(1)} %pad_add_fusion.base_ref, s32[3,64]{1,0:T(4,128)S(1)} %copy-done.4, f32[12,128,8]{2,1,0:T(8,128)S(1)} %get-tuple-element.13.columns_ref, f32[12,8,128]{2,1,0:T(8,128)S(1)} %get-tuple-element.14.rows_ref, f32[12,128,128]{2,1,0:T(8,128)S(1)} %get-tuple-element.19.mapped_ref, ...), custom_call_target="tpu_custom_call" | custom-call | tf_op jit(solution)/shard_map/pallas_call | solution.py:182
  119.3 34.5 %shard_map.77 = f32[128,512]{1,0:T(8,128)S(1)} custom-call(f32[12,128,128]{2,1,0:T(8,128)S(1)} %shard_map.76.collected_ref, f32[4,128,128]{2,1,0:T(8,128)S(1)} %get-tuple-element.20.state_ref, f32[8,4,2,64,128]{4,3,2,1,0:T(8,128)S(1)} %get-tuple-element.17.mix_ref), custom_call_target="tpu_custom_call" | custom-call | tf_op jit(solution)/shard_map/pallas_call | solution.py:489
  153.7 0.7 copy.9
  (1 shorter events, 0.0 us)
Async XLA Ops:
  2.4 1.0 copy-start
  3.4 1.0 copy-start.1
  4.4 0.9 copy-start.2
  48.0 0.7 copy-start.3
  61.8 44.3 %copy-start.4 = (s32[3,64]{1,0:T(4,128)S(1)}, s32[3,64]{1,0:T(4,128)}, u32[]{:S(2)}) copy-start(s32[3,64]{1,0:T(4,128)} %table_ref.3) | copy-start | bytes 2308

commit v4 on v3

--- a/solution.py
+++ b/solution.py
@@ -85,12 +85,15 @@
     rows_ref,
     mapped_ref,
     filter_ref,
+    turned_ref,
     out_ref,
     count_s,
     to_s,
     from_s,
     weight_s,
     operand_v,
+    scaled_v,
+    other_v,
     basis_a,
     basis_b,
 ):
@@ -121,17 +124,10 @@
     def list_row(first, n):
         def list_one(second, n):
             many = count_s[first * slots + second]
-            live = (many > 0).astype(jnp.int32)
-            other = live * (first != second).astype(jnp.int32)
-            weight = many.astype(jnp.float32)
             to_s[n] = first
             from_s[n] = second
-            weight_s[n] = weight
-            n = n + live
-            to_s[n] = second
-            from_s[n] = first
-            weight_s[n] = weight
-            return n + other
+            weight_s[n] = many.astype(jnp.float32)
+            return n + (many > 0).astype(jnp.int32)
 
         return lax.fori_loop(first, slots, list_one, n)
 
@@ -146,7 +142,14 @@
         for part in range(2):
             operand_v[slot, part * extent : (part + 1) * extent, :channels] = high
             operand_v[slot, part * extent : (part + 1) * extent, channels:] = low
+    for slot in range(blocks):
+        turned = mapped_ref[slot].T
+        for k in range(K):
+            high, low = split_halves(turned * turned_ref[:, k : k + 1])
+            scaled_v[slot, :channels, k * extent : (k + 1) * extent] = high
+            scaled_v[slot, channels:, k * extent : (k + 1) * extent] = low
     out_ref[...] = jnp.zeros_like(out_ref)
+    other_v[...] = jnp.zeros_like(other_v)
 
     def build(task, basis):
         to, source = to_s[task], from_s[task]
@@ -160,6 +163,10 @@
             part = product[k * extent : (k + 1) * extent]
             summed = summed + filter_ref[k : k + 1, :] * (part[:, :channels] + part[:, channels:])
         out_ref[to] = out_ref[to] + summed
+        both = jnp.dot(scaled_v[to], basis[...], preferred_element_type=jnp.float32)
+        back = both[:channels] + both[channels:]
+        back = back[:, :extent] + back[:, extent:]
+        other_v[source] = other_v[source] + back * jnp.where(to == source, 0.0, 1.0)
 
     build(0, basis_a)
 
@@ -172,17 +179,19 @@
         return carry
 
     lax.fori_loop(0, (total + 1) // 2, step, 0)
+    for slot in range(slots):
+        out_ref[slot] = out_ref[slot] + other_v[slot].T
 
 
 def pair_messages(base, table, columns, rows, mapped, filters, blocks, interpret=False):
     slots, extent, channels = mapped.shape
-    tasks = 2 * blocks * slots + 8
+    tasks = blocks * slots + 8
     smem = pl.BlockSpec(memory_space=pltpu.SMEM)
     vmem = pl.BlockSpec(memory_space=pltpu.VMEM)
     return pl.pallas_call(
         functools.partial(pair_kernel, blocks),
         out_shape=jax.ShapeDtypeStruct(mapped.shape, jnp.float32),
-        in_specs=[smem, smem, vmem, vmem, vmem, vmem],
+        in_specs=[smem, smem, vmem, vmem, vmem, vmem, vmem],
         out_specs=vmem,
         scratch_shapes=[
             pltpu.SMEM((blocks * slots,), jnp.int32),
@@ -190,12 +199,14 @@
             pltpu.SMEM((tasks,), jnp.int32),
             pltpu.SMEM((tasks,), jnp.float32),
             pltpu.VMEM((slots, 2 * extent, 2 * channels), jnp.bfloat16),
+            pltpu.VMEM((blocks, 2 * channels, K * extent), jnp.bfloat16),
+            pltpu.VMEM((slots, channels, extent), jnp.float32),
             pltpu.VMEM((K * extent, 2 * extent), jnp.bfloat16),
             pltpu.VMEM((K * extent, 2 * extent), jnp.bfloat16),
         ],
         compiler_params=pltpu.CompilerParams(vmem_limit_bytes=48 * 1024 * 1024),
         interpret=interpret,
-    )(base, table, columns, rows, mapped, filters)
+    )(base, table, columns, rows, mapped, filters, filters.T)
 
 
 HIGHEST = lax.Precision.HIGHEST
@@ -270,13 +281,21 @@
     all_mix_ref,
     all_in_ref,
     landed,
+    feature_v,
+    weight_v,
     *sems,
 ):
     place = greet(reach, 2)
     space, chan, spatial, groups = place
-    chan_sems, space_sems, near_sems, piece_sems, far_sems, pair_sems = (
-        sems[2 * i : 2 * i + 2] for i in range(6)
-    )
+    chan_sems, space_sems, near_sems, piece_sems, far_sems, pair_sems, own_sems = (
+        sems[2 * i : 2 * i + 2] for i in range(7)
+    )
+    fetched = [
+        pltpu.make_async_copy(feature_ref, feature_v, own_sems[0].at[0]),
+        pltpu.make_async_copy(weight_ref.at[0], weight_v, own_sems[0].at[1]),
+    ]
+    for copy in fetched:
+        copy.start()
     rows, _ = feature_ref.shape
     extent = out_ref.shape[1]
     blocks = geometry_ref.shape[0]
@@ -326,8 +345,12 @@
             )
 
     tell(0)
-    for held, target in shares:
-        target[space, chan] = held[...]
+    kept = []
+    for kind, (held, target) in enumerate(shares):
+        kept.append(pltpu.make_async_copy(held, target.at[space, chan], own_sems[1].at[kind]))
+        kept[-1].start()
+    for copy in kept:
+        copy.wait()
     for copy in pieces:
         copy.wait_recv()
     far, paired = [], []
@@ -350,6 +373,8 @@
         paired.append(send(target.at[space], target.at[space], pair_sems, (kind, 0), partner))
     for q in range(1, groups):
         tell(q)
+    for copy in fetched:
+        copy.wait()
     for q in range(groups):
         total = 0.0
         for p in range(groups):
@@ -357,14 +382,14 @@
                 arriving[p, q].wait_recv()
                 part = landed[p - 1, q]
             else:
-                part = feature_ref[:, q * extent : (q + 1) * extent]
+                part = feature_v[:, q * extent : (q + 1) * extent]
             source = lax.rem(chan + groups - p, groups)
             columns = pl.ds(pl.multiple_of(source * rows, rows), rows)
-            total = total + contract(weight_ref[0, :, columns], part, 1, 0)
+            total = total + contract(weight_v[:, columns], part, 1, 0)
         out_ref[q] = total.T
         leaving += spread_block(out_ref, q, q, reach, groups, place, space_sems)
     own = pl.ds(pl.multiple_of(chan * extent, extent), extent)
-    state_ref[chan] = feature_ref[:, own]
+    state_ref[chan] = feature_v[:, own]
     for p in range(1, groups):
         state_ref[lax.rem(chan + groups - p, groups)] = landed[p - 1, chan]
     for copy, kind, hop in far:
@@ -483,13 +508,14 @@
         copy.wait_send()
 
 
-def remote_call(kernel, outs, scratch, pairs, collective, *operands):
+def remote_call(kernel, outs, scratch, pairs, collective, *operands, elsewhere=0):
     vmem = pl.BlockSpec(memory_space=pltpu.VMEM)
     sems = [pltpu.SemaphoreType.DMA(shape) for shape in pairs for _ in range(2)]
     return pl.pallas_call(
         kernel,
         out_shape=[jax.ShapeDtypeStruct(shape, jnp.float32) for shape in outs],
-        in_specs=[vmem] * len(operands),
+        in_specs=[vmem] * (len(operands) - elsewhere)
+        + [pl.BlockSpec(memory_space=pl.ANY)] * elsewhere,
         out_specs=[vmem] * len(outs),
         scratch_shapes=[pltpu.VMEM(shape, jnp.float32) for shape in scratch] + sems,
         compiler_params=pltpu.CompilerParams(
@@ -519,7 +545,7 @@
             (spatial, groups, LAYERS, mix_part, mix_weight.shape[2]),
             (spatial, groups, LAYERS - 1, in_part, in_weight.shape[2]),
         ],
-        [(groups - 1, groups, channels, block_len)],
+        [(groups - 1, groups, channels, block_len), features.shape, in_weight.shape[1:]],
         [
             (groups - 1, groups),
             (reach, groups),
@@ -527,12 +553,14 @@
             (2, groups - 1),
             (2, hops - 1),
             (2, hops),
+            (2,),
         ],
         0,
         geometry,
         features,
         in_weight,
         mix_weight,
+        elsewhere=3,
     )
     scratch = [(reach, groups, *square), (groups, *square), (groups - 1, *square)]
     for layer in range(LAYERS - 1):

time: 155 us -> 144 us (0.929); the launches traced: 154 us -> 142 us
  Pallas kernels: 148 us -> 130 us
  local copies, waits for them, and re-layouts: 5.2 us -> 10.5 us
    pallas_call x3, Pallas kernels: 121 us -> 104 us  [remote_call(): pl.pallas_call(kernel, out_shape=[jax.ShapeDtypeStruct(shape, jnp.float32...]
    unnamed x11 -> x25, local copies, waits for them, and re-layouts: 4.42 us -> 9.76 us
where the time goes in v4:
time: 144 us; the launch traced here: 142 us
  Pallas kernels  130 us (90%)
  local copies, waits for them, and re-layouts  10.5 us (7%)
  other arithmetic  1.57 us (1%)
    pallas_call x3, Pallas kernels, remote_call(): pl.pallas_call(kernel, out_shape=[jax.ShapeDtypeStruct(shape, jnp.float32...  104 us
    pallas_call x2, Pallas kernels, pair_messages(): pl.pallas_call(functools.partial(pair_kernel, blocks), out_shape=jax.Shap...  25 us
    unnamed x25, local copies, waits for them, and re-layouts  9.76 us

profile of v4, /device:TPU:0, one launch (start us, length us, event | category | flops | bytes accessed | tf_op | source)
XLA Modules:
  0.0 141.7 jit_solution(17540489513841548544)
XLA Ops:
  0.0 0.7 compare_convert_fusion
  0.7 0.1 pad.2.clone
  0.8 0.8 maximum_bitcast_fusion.geometry_ref
  1.6 0.0 copy-start.6
  1.6 1.0 copy-done.6
  2.6 0.0 copy-start.7
  2.6 1.0 copy-done.7
  3.7 0.0 copy-start.8
  3.7 0.9 copy-done.8
  4.6 42.7 %shard_map.73 = (f32[12,128,128]{2,1,0:T(8,128)S(1)}, f32[4,128,128]{2,1,0:T(8,128)S(1)}, f32[12,8,128]{2,1,0:T(8,128)S(1)}, f32[12,128,8]{2,1,0:T(8,128)S(1)}, ...) custom-call(f32[4,8,128]{2,1,0:T(8,128)S(1)} %maximum_bitcast_fusion.geometry_ref, ...), custom_call_target="tpu_custom_call" | custom-call | tf_op jit(solution)/shard_map/pallas_call | solution.py:514
  47.3 0.0 copy-start
  47.3 1.0 copy-done
  48.3 0.0 copy-start.2
  48.3 0.9 copy-done.2
  49.2 0.7 fusion
  49.9 0.1 copy.12
  50.0 0.1 pad_add_fusion.base_ref
  50.1 1.2 copy-done.3
  51.3 0.7 copy-done.9
  52.0 12.5 %shard_map.74.collected_ref = f32[12,128,128]{2,1,0:T(8,128)S(1)} custom-call(s32[2]{0:T(128)S(1)} %pad_add_fusion.base_ref, s32[3,64]{1,0:T(4,128)S(1)} %copy-done.9, f32[12,128,8]{2,1,0:T(8,128)S(1)} %get-tuple-element.13.columns_ref, f32[12,8,128]{2,1,0:T(8,128)S(1)} %get-tuple-element.14.rows_ref, f32[12,128,128]{2,1,0:T(8,128)S(1)} %copy-done.3, ...), custom_call_target="tpu_custom_call" | custom-call | tf_op jit(solution)/shard_map/pallas_call | solution.py:191
  64.5 0.0 copy-done.1
  64.5 0.0 copy-start.10
  64.5 35.8 %shard_map.75 = (f32[12,128,128]{2,1,0:T(8,128)S(1)}, f32[4,128,128]{2,1,0:T(8,128)S(1)}) custom-call(f32[12,128,128]{2,1,0:T(8,128)S(1)} %shard_map.74.collected_ref, f32[4,128,128]{2,1,0:T(8,128)S(1)} %get-tuple-element.16.state_ref, f32[8,4,2,64,128]{4,3,2,1,0:T(8,128)S(1)} %get-tuple-element.17.mix_ref, f32[8,4,1,16,512]{4,3,2,1,0:T(8,128)S(1)} %copy-done.1), custom_call_target="tpu_custom_call" | custom-call | tf_op jit(solution)/shard_map/pallas_call | solution.py:514
  100.4 0.0 copy-start.4
  100.4 0.9 copy-done.4
  101.3 0.1 copy.13
  101.4 0.0 copy-done.10
  101.4 0.0 copy-start.5
  101.4 1.1 copy-done.5
  102.5 12.5 %shard_map.76.collected_ref = f32[12,128,128]{2,1,0:T(8,128)S(1)} custom-call(s32[2]{0:T(128)S(1)} %pad_add_fusion.base_ref, s32[3,64]{1,0:T(4,128)S(1)} %copy-done.10, f32[12,128,8]{2,1,0:T(8,128)S(1)} %get-tuple-element.13.columns_ref, f32[12,8,128]{2,1,0:T(8,128)S(1)} %get-tuple-element.14.rows_ref, f32[12,128,128]{2,1,0:T(8,128)S(1)} %copy-done.5, ...), custom_call_target="tpu_custom_call" | custom-call | tf_op jit(solution)/shard_map/pallas_call | solution.py:191
  115.0 26.0 %shard_map.77 = f32[128,512]{1,0:T(8,128)S(1)} custom-call(f32[12,128,128]{2,1,0:T(8,128)S(1)} %shard_map.76.collected_ref, f32[4,128,128]{2,1,0:T(8,128)S(1)} %get-tuple-element.20.state_ref, f32[8,4,2,64,128]{4,3,2,1,0:T(8,128)S(1)} %get-tuple-element.17.mix_ref), custom_call_target="tpu_custom_call" | custom-call | tf_op jit(solution)/shard_map/pallas_call | solution.py:514
  141.0 0.7 copy.17
  (4 shorter events, 0.0 us)
Async XLA Ops:
  1.6 1.0 copy-start.6
  2.6 1.0 copy-start.7
  3.7 0.9 copy-start.8
  47.3 1.0 copy-start
  48.3 0.9 copy-start.2
  50.0 14.5 %copy-start.1 = (f32[8,4,1,16,512]{4,3,2,1,0:T(8,128)S(1)}, f32[8,4,1,16,512]{4,3,2,1,0:T(8,128)}, u32[]{:S(2)}) copy-start(f32[8,4,1,16,512]{4,3,2,1,0:T(8,128)} %copy-done) | copy-start | bytes 3145732
  50.1 1.2 copy-start.3
  51.3 0.7 copy-start.9
  64.5 36.9 %copy-start.10 = (s32[3,64]{1,0:T(4,128)S(1)}, s32[3,64]{1,0:T(4,128)}, u32[]{:S(2)}) copy-start(s32[3,64]{1,0:T(4,128)} %table_ref.3) | copy-start | bytes 2308
  100.4 0.9 copy-start.4
  101.4 1.1 copy-start.5

commit v5 on v4

--- a/solution.py
+++ b/solution.py
@@ -204,7 +204,7 @@
             pltpu.VMEM((K * extent, 2 * extent), jnp.bfloat16),
             pltpu.VMEM((K * extent, 2 * extent), jnp.bfloat16),
         ],
-        compiler_params=pltpu.CompilerParams(vmem_limit_bytes=48 * 1024 * 1024),
+        compiler_params=pltpu.CompilerParams(vmem_limit_bytes=60 * 1024 * 1024),
         interpret=interpret,
     )(base, table, columns, rows, mapped, filters, filters.T)
 
@@ -266,6 +266,54 @@
             )
         )
     return copies
+
+
+class Line:
+    def __init__(self, place, sems):
+        self.space, self.chan, _, self.groups = place
+        self.sems = sems
+        self.sent = []
+        near = [p for far in range(1, self.groups) for p in (far, self.groups - far)]
+        self.order = list(dict.fromkeys(near))
+
+    def hand(self, source, target, owner, at, send_at, step, when):
+        copy = pltpu.make_async_remote_copy(
+            src_ref=source,
+            dst_ref=target,
+            send_sem=self.sems[0].at[(send_at, *at)],
+            recv_sem=self.sems[1].at[(owner, *at)],
+            device_id=(self.space, lax.rem(self.chan + self.groups + step, self.groups)),
+            device_id_type=MESH,
+        )
+        pl.when(when)(copy.start)
+        self.sent.append((copy, when))
+
+    def begin(self, source, target, at):
+        chan, last = self.chan, self.groups - 1
+        self.hand(source, target, chan, at, chan, 1, chan < last)
+        self.hand(source, target, chan, at, self.groups, -1, chan > 0)
+
+    def take(self, target_of, at):
+        chan, last = self.chan, self.groups - 1
+        for p in self.order:
+            owner = lax.rem(chan + self.groups - p, self.groups)
+            target = target_of(owner)
+            pltpu.make_async_remote_copy(
+                src_ref=target,
+                dst_ref=target,
+                send_sem=self.sems[0].at[(owner, *at)],
+                recv_sem=self.sems[1].at[(owner, *at)],
+                device_id=(self.space, owner),
+                device_id_type=MESH,
+            ).wait_recv()
+            up = (owner < chan) & (chan < last)
+            down = (owner > chan) & (chan > 0)
+            self.hand(target, target, owner, at, owner, 1, up)
+            self.hand(target, target, owner, at, owner, -1, down)
+
+    def finish(self):
+        for copy, when in self.sent:
+            pl.when(when)(copy.wait_send)
 
 
 def gather_kernel(
@@ -309,18 +357,10 @@
         else:
             held = source.at[:, mine]
         shares.append((held, target))
-    pieces, leaving = [], []
-    for p in range(1, groups):
-        for kind, (held, target) in enumerate(shares):
-            pieces.append(
-                send(
-                    held,
-                    target.at[space, chan],
-                    piece_sems,
-                    (kind, p - 1),
-                    (space, lax.rem(chan + p, groups)),
-                )
-            )
+    leaving = []
+    pieces, chunks = Line(place, piece_sems), Line(place, chan_sems)
+    for kind, (held, target) in enumerate(shares):
+        pieces.begin(held, target.at[space, chan], (kind,))
     rows_ref[:blocks] = geometry_ref[...]
     for offset in range(1, reach + 1):
         leaving.append(
@@ -332,27 +372,16 @@
                 (lax.rem(space + spatial - offset, spatial), chan),
             )
         )
-    arriving = {}
-
-    def tell(q):
-        for p in range(1, groups):
-            arriving[p, q] = send(
-                feature_ref.at[:, q * extent : (q + 1) * extent],
-                landed.at[p - 1, q],
-                chan_sems,
-                (p - 1, q),
-                (space, lax.rem(chan + p, groups)),
-            )
-
-    tell(0)
+    for q in range(groups):
+        chunks.begin(feature_ref.at[:, q * extent : (q + 1) * extent], landed.at[chan, q], (q,))
     kept = []
     for kind, (held, target) in enumerate(shares):
         kept.append(pltpu.make_async_copy(held, target.at[space, chan], own_sems[1].at[kind]))
         kept[-1].start()
     for copy in kept:
         copy.wait()
-    for copy in pieces:
-        copy.wait_recv()
+    for kind, (_, target) in enumerate(shares):
+        pieces.take(lambda owner, target=target: target.at[space, owner], (kind,))
     far, paired = [], []
     partner = (space + 1 - 2 * lax.rem(space, 2), chan)
     for kind, (_, target) in enumerate(shares):
@@ -371,19 +400,17 @@
                 )
             )
         paired.append(send(target.at[space], target.at[space], pair_sems, (kind, 0), partner))
-    for q in range(1, groups):
-        tell(q)
     for copy in fetched:
         copy.wait()
     for q in range(groups):
+        chunks.take(lambda owner, q=q: landed.at[owner, q], (q,))
         total = 0.0
         for p in range(groups):
+            source = lax.rem(chan + groups - p, groups)
             if p > 0:
-                arriving[p, q].wait_recv()
-                part = landed[p - 1, q]
+                part = landed[source, q]
             else:
                 part = feature_v[:, q * extent : (q + 1) * extent]
-            source = lax.rem(chan + groups - p, groups)
             columns = pl.ds(pl.multiple_of(source * rows, rows), rows)
             total = total + contract(weight_v[:, columns], part, 1, 0)
         out_ref[q] = total.T
@@ -391,7 +418,8 @@
     own = pl.ds(pl.multiple_of(chan * extent, extent), extent)
     state_ref[chan] = feature_v[:, own]
     for p in range(1, groups):
-        state_ref[lax.rem(chan + groups - p, groups)] = landed[p - 1, chan]
+        source = lax.rem(chan + groups - p, groups)
+        state_ref[source] = landed[source, chan]
     for copy, kind, hop in far:
         copy.wait_recv()
         source = lax.rem(space + spatial - 2 * hop, spatial)
@@ -401,8 +429,10 @@
         copy.wait()
     for at in range(rows_ref.shape[0]):
         columns_ref[at] = rows_ref[at].T
-    for copy in list(arriving.values()) + pieces + [copy for copy, _, _ in far]:
+    for copy, _, _ in far:
         copy.wait_send()
+    pieces.finish()
+    chunks.finish()
 
 
 def mix_states(reach, layer, collected_ref, state_ref, mix_ref, back, sums, heard, place, back_sems, sum_sems):
@@ -519,7 +549,7 @@
         out_specs=[vmem] * len(outs),
         scratch_shapes=[pltpu.VMEM(shape, jnp.float32) for shape in scratch] + sems,
         compiler_params=pltpu.CompilerParams(
-            collective_id=collective, has_side_effects=True, vmem_limit_bytes=40 * 1024 * 1024
+            collective_id=collective, has_side_effects=True, vmem_limit_bytes=60 * 1024 * 1024
         ),
     )(*operands)
 
@@ -545,12 +575,12 @@
             (spatial, groups, LAYERS, mix_part, mix_weight.shape[2]),
             (spatial, groups, LAYERS - 1, in_part, in_weight.shape[2]),
         ],
-        [(groups - 1, groups, channels, block_len), features.shape, in_weight.shape[1:]],
+        [(groups, groups, channels, block_len), features.shape, in_weight.shape[1:]],
         [
-            (groups - 1, groups),
+            (groups + 1, groups),
             (reach, groups),
             (reach,),
-            (2, groups - 1),
+            (groups + 1, 2),
             (2, hops - 1),
             (2, hops),
             (2,),

time: 144 us -> 156 us (1.083)
  Pallas kernels: 130 us -> 148 us
  local copies, waits for them, and re-layouts: 10.5 us -> 4.51 us
    pallas_call x3, Pallas kernels: 104 us -> 115 us  [remote_call(): pl.pallas_call(kernel, out_shape=[jax.ShapeDtypeStruct(shape, jnp.float32...]
    pallas_call x2, Pallas kernels: 25 us -> 32.3 us  [pair_messages(): pl.pallas_call(functools.partial(pair_kernel, blocks), out_shape=jax.Shap...]
    unnamed x25 -> x3, local copies, waits for them, and re-layouts: 9.76 us -> 3.13 us
where the time goes in v5:
time: 156 us; the launch traced here: 155 us
  Pallas kernels  148 us (95%)
  local copies, waits for them, and re-layouts  4.51 us (3%)
  other arithmetic  2.68 us (2%)
    pallas_call x3, Pallas kernels, remote_call(): pl.pallas_call(kernel, out_shape=[jax.ShapeDtypeStruct(shape, jnp.float32...  115 us
    pallas_call x2, Pallas kernels, pair_messages(): pl.pallas_call(functools.partial(pair_kernel, blocks), out_shape=jax.Shap...  32.3 us
    unnamed x3, local copies, waits for them, and re-layouts  3.13 us

profile of v5, /device:TPU:0, one launch (start us, length us, event | category | flops | bytes accessed | tf_op | source)
XLA Modules:
  0.0 154.8 jit_solution(15353618986486276073)
XLA Ops:
  0.0 0.7 compare_convert_fusion
  0.7 0.1 pad.2.clone
  0.8 1.4 maximum_bitcast_fusion.geometry_ref
  2.2 51.0 %shard_map.73 = (f32[12,128,128]{2,1,0:T(8,128)}, f32[4,128,128]{2,1,0:T(8,128)}, f32[12,8,128]{2,1,0:T(8,128)}, f32[12,128,8]{2,1,0:T(8,128)}, f32[8,4,2,64,128...) custom-call(f32[4,8,128]{2,1,0:T(8,128)} %maximum_bitcast_fusion.geometry_ref, f32[128,512]{1,0:T(8,128)} %feature_ref.1, ...), custom_call_target="tpu_custom_call" | custom-call | tf_op jit(solution)/shard_map/pallas_call | solution.py:544
  53.2 1.3 fusion
  54.5 0.7 copy.12
  55.2 0.6 pad_add_fusion.base_ref
  55.8 16.1 %shard_map.74.collected_ref = f32[12,128,128]{2,1,0:T(8,128)} custom-call(s32[2]{0:T(128)} %pad_add_fusion.base_ref, s32[3,64]{1,0:T(4,128)} %table_ref.3, f32[12,128,8]{2,1,0:T(8,128)} %get-tuple-element.13.columns_ref, f32[12,8,128]{2,1,0:T(8,128)} %get-tuple-element.14.rows_ref, f32[12,128,128]{2,1,0:T(8,128)} %get-tuple-element.15.mapped_ref, ...), custom_call_target="tpu_custom_call" | custom-call | tf_op jit(solution)/shard_map/pallas_call | solution.py:191
  71.9 34.2 %shard_map.75 = (f32[12,128,128]{2,1,0:T(8,128)}, f32[4,128,128]{2,1,0:T(8,128)}) custom-call(f32[12,128,128]{2,1,0:T(8,128)} %shard_map.74.collected_ref, f32[4,128,128]{2,1,0:T(8,128)} %get-tuple-element.16.state_ref, f32[8,4,2,64,128]{4,3,2,1,0:T(8,128)} %get-tuple-element.17.mix_ref, f32[8,4,1,16,512]{4,3,2,1,0:T(8,128)} %get-tuple-element.18.in_ref), custom_call_target="tpu_custom_call" | custom-call | tf_op jit(solution)/shard_map/pallas_call | solution.py:544
  106.1 0.7 copy.13
  106.9 16.1 %shard_map.76.collected_ref = f32[12,128,128]{2,1,0:T(8,128)} custom-call(s32[2]{0:T(128)} %pad_add_fusion.base_ref, s32[3,64]{1,0:T(4,128)} %table_ref.3, f32[12,128,8]{2,1,0:T(8,128)} %get-tuple-element.13.columns_ref, f32[12,8,128]{2,1,0:T(8,128)} %get-tuple-element.14.rows_ref, f32[12,128,128]{2,1,0:T(8,128)} %get-tuple-element.19.mapped_ref, ...), custom_call_target="tpu_custom_call" | custom-call | tf_op jit(solution)/shard_map/pallas_call | solution.py:191
  123.0 30.1 %shard_map.77 = f32[128,512]{1,0:T(8,128)} custom-call(f32[12,128,128]{2,1,0:T(8,128)} %shard_map.76.collected_ref, f32[4,128,128]{2,1,0:T(8,128)} %get-tuple-element.20.state_ref, f32[8,4,2,64,128]{4,3,2,1,0:T(8,128)} %get-tuple-element.17.mix_ref), custom_call_target="tpu_custom_call" | custom-call | tf_op jit(solution)/shard_map/pallas_call | solution.py:544
  153.1 1.7 %copy.17 = f32[128,512]{1,0:T(8,128)} copy(f32[128,512]{1,0:T(8,128)} %shard_map.77) | data formatting | bytes 524288
  (1 shorter events, 0.0 us)

commit v6 on v4

--- a/solution.py
+++ b/solution.py
@@ -304,10 +304,8 @@
     for source, target in ((mix_ref, all_mix_ref), (weight_ref, all_in_ref)):
         part = target.shape[-2]
         mine = pl.ds(pl.multiple_of(space * part, part), part)
-        if target is all_in_ref:
-            held = source.at[pl.ds(1, LAYERS - 1), mine]
-        else:
-            held = source.at[:, mine]
+        first_layer = 1 if target is all_in_ref else 0
+        held = source.at[pl.ds(first_layer, LAYERS - 1), mine]
         shares.append((held, target))
     pieces, leaving = [], []
     for p in range(1, groups):
@@ -508,7 +506,7 @@
         copy.wait_send()
 
 
-def remote_call(kernel, outs, scratch, pairs, collective, *operands, elsewhere=0):
+def remote_call(kernel, outs, scratch, pairs, collective, *operands, elsewhere=0, grant=40):
     vmem = pl.BlockSpec(memory_space=pltpu.VMEM)
     sems = [pltpu.SemaphoreType.DMA(shape) for shape in pairs for _ in range(2)]
     return pl.pallas_call(
@@ -519,9 +517,17 @@
         out_specs=[vmem] * len(outs),
         scratch_shapes=[pltpu.VMEM(shape, jnp.float32) for shape in scratch] + sems,
         compiler_params=pltpu.CompilerParams(
-            collective_id=collective, has_side_effects=True, vmem_limit_bytes=40 * 1024 * 1024
+            collective_id=collective, has_side_effects=True, vmem_limit_bytes=grant * 1024 * 1024
         ),
     )(*operands)
+
+
+def all_pieces(local):
+    spatial = lax.axis_size("space")
+    part = local.shape[0] // spatial
+    share = lax.dynamic_slice_in_dim(local, lax.axis_index("space") * part, part, 0)
+    gathered = lax.all_gather(share, ("space", "chan"), axis=0, tiled=False)
+    return gathered.reshape(spatial, lax.axis_size("chan"), 1, part, local.shape[1])
 
 
 def exchanged_layers(geometry, features, in_weight, mix_weight, reach, pairs_of):
@@ -535,6 +541,7 @@
     hops = spatial // 2
     mix_part = mix_weight.shape[1] // spatial
     in_part = in_weight.shape[1] // spatial
+    last_mix = all_pieces(mix_weight[LAYERS - 1])
     mapped, state, rows, columns, all_mix, all_in = remote_call(
         functools.partial(gather_kernel, reach),
         [
@@ -542,7 +549,7 @@
             held,
             (slots, 8, block_len),
             (slots, block_len, 8),
-            (spatial, groups, LAYERS, mix_part, mix_weight.shape[2]),
+            (spatial, groups, LAYERS - 1, mix_part, mix_weight.shape[2]),
             (spatial, groups, LAYERS - 1, in_part, in_weight.shape[2]),
         ],
         [(groups - 1, groups, channels, block_len), features.shape, in_weight.shape[1:]],
@@ -561,6 +568,7 @@
         in_weight,
         mix_weight,
         elsewhere=3,
+        grant=60,
     )
     scratch = [(reach, groups, *square), (groups, *square), (groups - 1, *square)]
     for layer in range(LAYERS - 1):
@@ -578,14 +586,14 @@
         )
     collected = pairs_of(columns, rows, mapped, LAYERS - 1)
     (updated,) = remote_call(
-        functools.partial(last_kernel, reach, LAYERS - 1),
+        functools.partial(last_kernel, reach, 0),
         [features.shape],
         scratch + [held],
         [(reach, groups), (groups - 1,), (groups - 1,)],
         2,
         collected,
         state,
-        all_mix,
+        last_mix,
     )
     return updated
 

time: 144 us -> 156 us (1.083); the launches traced: 142 us -> 157 us
  between operations: 0.1 us -> 13.5 us
  Pallas kernels: 130 us -> 134 us
  local copies, waits for them, and re-layouts: 10.5 us -> 8.75 us
    pallas_call x2, Pallas kernels: 25 us -> 34.1 us  [pair_messages(): pl.pallas_call(functools.partial(pair_kernel, blocks), out_shape=jax.Shap...]
    pallas_call x3, Pallas kernels: 104 us -> 99.4 us  [remote_call(): pl.pallas_call(kernel, out_shape=[jax.ShapeDtypeStruct(shape, jnp.float32...]
    unnamed x25 -> x29, local copies, waits for them, and re-layouts: 9.76 us -> 7.11 us
  transfers between devices with their start and end apart: 0 -> 1, of which waited for: 0 -> 0; matrix products, arithmetic and copies ran while one was open for 0% -> 1% of each run, Pallas kernels for 0% -> 70%
where the time goes in v6:
time: 156 us; the launch traced here: 157 us
  Pallas kernels  134 us (86%)
  between operations  13.5 us (9%)
  local copies, waits for them, and re-layouts  8.75 us (6%)
    pallas_call x3, Pallas kernels, remote_call(): pl.pallas_call(kernel, out_shape=[jax.ShapeDtypeStruct(shape, jnp.float32...  99.4 us
    pallas_call x2, Pallas kernels, pair_messages(): pl.pallas_call(functools.partial(pair_kernel, blocks), out_shape=jax.Shap...  34.1 us
    unnamed x29, local copies, waits for them, and re-layouts  7.11 us
  transfers between devices with their start and end apart: 1, of which 0 were waited for; matrix products, arithmetic and copies ran while one was open for 1% of the time, Pallas kernels for 70%

profile of v6, /device:TPU:0, one launch (start us, length us, event | category | flops | bytes accessed | tf_op | source)
XLA Modules:
  0.0 156.7 jit_solution(11659179422292965897)
XLA Ops:
  6.5 0.0 all-gather.2.cloned.1.call-start
  6.5 0.9 slice-done
  7.5 0.6 constant_dynamic-slice_fusion
  8.1 0.0 all-gather.2.cloned.1.call-update
  8.1 0.7 copy-done.10
  8.8 0.1 copy.16
  8.9 0.1 copy.17
  9.0 0.1 pad.2.clone
  9.1 0.5 copy-done.12
  9.6 0.1 compare_convert_fusion
  9.6 0.1 copy-done.11
  9.7 0.7 maximum_bitcast_fusion.geometry_ref
  10.4 44.1 %shard_map.73 = (f32[12,128,128]{2,1,0:T(8,128)}, f32[4,128,128]{2,1,0:T(8,128)}, f32[12,8,128]{2,1,0:T(8,128)}, f32[12,128,8]{2,1,0:T(8,128)}, f32[8,4,1,64,128...) custom-call(f32[4,8,128]{2,1,0:T(8,128)} %maximum_bitcast_fusion.geometry_ref, f32[128,512]{1,0:T(8,128)} %feature_ref.1, ...), custom_call_target="tpu_custom_call" | custom-call | tf_op jit(solution)/shard_map/pallas_call | solution.py:512
  54.5 0.1 pad_add_fusion.base_ref
  54.6 0.7 copy-done.9
  55.3 1.1 copy-done
  56.4 1.1 copy-done.5
  57.5 0.8 copy-done.7
  58.3 17.1 %shard_map.74.collected_ref = f32[12,128,128]{2,1,0:T(8,128)S(1)} custom-call(s32[2]{0:T(128)S(1)} %pad_add_fusion.base_ref, s32[3,64]{1,0:T(4,128)S(1)} %copy-done.9, f32[12,128,8]{2,1,0:T(8,128)S(1)} %copy-done, f32[12,8,128]{2,1,0:T(8,128)S(1)} %copy-done.7, f32[12,128,128]{2,1,0:T(8,128)S(1)} %copy-done.5, f32[8,128]{1,0:T(8,128)S(1)} %get-tuple-element.22.filter_ref, ...), custom_call_target="tpu_custom_call" | custom-call | tf_op jit(solution)/shard_map/pallas_call | solution.py:191
  75.4 0.0 copy-done.2
  75.4 0.0 copy-done.3
  75.4 0.0 copy-done.6
  75.5 0.0 copy-start.1
  75.5 0.0 copy-start.8
  75.5 31.2 %shard_map.75 = (f32[12,128,128]{2,1,0:T(8,128)S(1)}, f32[4,128,128]{2,1,0:T(8,128)S(1)}) custom-call(f32[12,128,128]{2,1,0:T(8,128)S(1)} %shard_map.74.collected_ref, f32[4,128,128]{2,1,0:T(8,128)S(1)} %copy-done.6, f32[8,4,1,64,128]{4,3,2,1,0:T(8,128)S(1)} %copy-done.2, f32[8,4,1,16,512]{4,3,2,1,0:T(8,128)S(1)} %copy-done.3), custom_call_target="tpu_custom_call" | custom-call | tf_op jit(solution)/shard_map/pallas_call | solution.py:512
  106.7 0.0 copy-done.1
  106.7 0.0 copy-done.8
  106.7 17.1 %shard_map.76.collected_ref = f32[12,128,128]{2,1,0:T(8,128)S(1)} custom-call(s32[2]{0:T(128)S(1)} %pad_add_fusion.base_ref, s32[3,64]{1,0:T(4,128)S(1)} %copy-done.9, f32[12,128,8]{2,1,0:T(8,128)S(1)} %copy-done.1, f32[12,8,128]{2,1,0:T(8,128)S(1)} %copy-done.8, f32[12,128,128]{2,1,0:T(8,128)S(1)} %get-tuple-element.19.mapped_ref, ...), custom_call_target="tpu_custom_call" | custom-call | tf_op jit(solution)/shard_map/pallas_call | solution.py:191
  123.8 0.0 all-gather.2.cloned.1.call-done
  123.8 1.2 copy-done.4
  125.0 24.1 %shard_map.77 = f32[128,512]{1,0:T(8,128)S(1)} custom-call(f32[12,128,128]{2,1,0:T(8,128)S(1)} %shard_map.76.collected_ref, f32[4,128,128]{2,1,0:T(8,128)S(1)} %get-tuple-element.20.state_ref, f32[8,4,1,64,128]{4,3,2,1,0:T(8,128)S(1)} %bitcast.15), custom_call_target="tpu_custom_call" | custom-call | tf_op jit(solution)/shard_map/pallas_call | solution.py:512
  149.1 0.7 copy.21
  (14 shorter events, 0.0 us)
Async XLA Ops:
  6.5 117.2 %all-gather.2.cloned.1.call-start = ((), (), s32[]{:S(2)}) async-start(), calls=%async_computation | async-start | bytes 1081344 | tf_op jit(solution)/shard_map/all_gather | solution.py:529
  6.5 0.9 slice-start
  8.1 0.7 copy-start.10
  8.9 0.7 copy-start.12
  9.0 0.7 copy-start.11
  54.6 0.7 copy-start.9
  55.3 1.1 copy-start
  56.4 1.1 copy-start.5
  57.5 0.8 copy-start.7
  58.3 17.1 %copy-start.2 = (f32[8,4,1,64,128]{4,3,2,1,0:T(8,128)S(1)}, f32[8,4,1,64,128]{4,3,2,1,0:T(8,128)}, u32[]{:S(2)}) copy-start(f32[8,4,1,64,128]{4,3,2,1,0:T(8,128)} %get-tuple-element.17.mix_ref) | copy-start | bytes 3145732
  58.3 17.1 %copy-start.3 = (f32[8,4,1,16,512]{4,3,2,1,0:T(8,128)S(1)}, f32[8,4,1,16,512]{4,3,2,1,0:T(8,128)}, u32[]{:S(2)}) copy-start(f32[8,4,1,16,512]{4,3,2,1,0:T(8,128)} %get-tuple-element.18.in_ref) | copy-start | bytes 3145732
  58.3 17.1 %copy-start.6 = (f32[4,128,128]{2,1,0:T(8,128)S(1)}, f32[4,128,128]{2,1,0:T(8,128)}, u32[]{:S(2)}) copy-start(f32[4,128,128]{2,1,0:T(8,128)} %get-tuple-element.16.state_ref) | copy-start | bytes 786436
  75.5 31.2 %copy-start.1 = (f32[12,128,8]{2,1,0:T(8,128)S(1)}, f32[12,128,8]{2,1,0:T(8,128)}, u32[]{:S(2)}) copy-start(f32[12,128,8]{2,1,0:T(8,128)} %get-tuple-element.13.columns_ref) | copy-start | bytes 147460
  75.5 31.2 %copy-start.8 = (f32[12,8,128]{2,1,0:T(8,128)S(1)}, f32[12,8,128]{2,1,0:T(8,128)}, u32[]{:S(2)}) copy-start(f32[12,8,128]{2,1,0:T(8,128)} %get-tuple-element.14.rows_ref) | copy-start | bytes 147460
  123.8 1.2 copy-start.4
Sparse Core Ops, SparseCore 0:
  10.3 58.1 all-gather.1

commit v7 on v4

--- a/solution.py
+++ b/solution.py
@@ -209,18 +209,20 @@
     )(base, table, columns, rows, mapped, filters, filters.T)
 
 
-HIGHEST = lax.Precision.HIGHEST
 MESH = pl.DeviceIdType.MESH
 
 
 def contract(left, right, left_dim, right_dim):
-    return lax.dot_general(
-        left,
-        right,
-        (((left_dim,), (right_dim,)), ((), ())),
-        precision=HIGHEST,
-        preferred_element_type=jnp.float32,
-    )
+    left, right = split_halves(left), split_halves(right)
+    total = 0.0
+    for one, other in ((0, 0), (0, 1), (1, 0)):
+        total = total + lax.dot_general(
+            left[one],
+            right[other],
+            (((left_dim,), (right_dim,)), ((), ())),
+            preferred_element_type=jnp.float32,
+        )
+    return total
 
 
 def greet(reach, stride=None):
@@ -254,18 +256,42 @@
 
 def spread_block(out_ref, block, p, reach, blocks, place, sems):
     space, chan, spatial, groups = place
-    copies = []
+    copies = {}
     for offset in range(1, reach + 1):
-        copies.append(
-            send(
-                out_ref.at[block],
-                out_ref.at[offset * blocks + block],
-                sems,
-                (offset - 1, p),
-                (lax.rem(space + spatial - offset, spatial), chan),
+        copies[offset] = pltpu.make_async_remote_copy(
+            src_ref=out_ref.at[block],
+            dst_ref=out_ref.at[offset * blocks + block],
+            send_sem=sems[0].at[offset - 1, p],
+            recv_sem=sems[1].at[offset - 1, p],
+            device_id=(lax.rem(space + spatial - offset, spatial), chan),
+            device_id_type=MESH,
+        )
+        if offset == 1 and reach > 1:
+            pl.when(lax.rem(space, 2) == 1)(copies[offset].start)
+        else:
+            copies[offset].start()
+    return [(block, p, copies)]
+
+
+def finish_blocks(out_ref, leaving, reach, blocks, place, sems):
+    space, chan, spatial, groups = place
+    for block, p, copies in leaving:
+        if reach > 1:
+            copies[2].wait_recv()
+            onward = pltpu.make_async_remote_copy(
+                src_ref=out_ref.at[2 * blocks + block],
+                dst_ref=out_ref.at[blocks + block],
+                send_sem=sems[0].at[0, p],
+                recv_sem=sems[1].at[0, p],
+                device_id=(lax.rem(space + 1, spatial), chan),
+                device_id_type=MESH,
             )
-        )
-    return copies
+            pl.when(lax.rem(space, 2) == 0)(onward.start)
+    for block, p, copies in leaving:
+        for offset, copy in copies.items():
+            if offset != 2:
+                copy.wait_recv()
+            copy.wait_send()
 
 
 def gather_kernel(
@@ -309,7 +335,7 @@
         else:
             held = source.at[:, mine]
         shares.append((held, target))
-    pieces, leaving = [], []
+    pieces, leaving, shifts = [], [], []
     for p in range(1, groups):
         for kind, (held, target) in enumerate(shares):
             pieces.append(
@@ -323,7 +349,7 @@
             )
     rows_ref[:blocks] = geometry_ref[...]
     for offset in range(1, reach + 1):
-        leaving.append(
+        shifts.append(
             send(
                 geometry_ref,
                 rows_ref.at[pl.ds(offset * blocks, blocks)],
@@ -397,7 +423,8 @@
         source = lax.rem(space + spatial - 2 * hop, spatial)
         target = shares[kind][1]
         paired.append(send(target.at[source], target.at[source], pair_sems, (kind, hop), partner))
-    for copy in leaving + paired:
+    finish_blocks(out_ref, leaving, reach, groups, place, space_sems)
+    for copy in shifts + paired:
         copy.wait()
     for at in range(rows_ref.shape[0]):
         columns_ref[at] = rows_ref[at].T
@@ -482,10 +509,9 @@
         handing[p].wait_recv()
         block = lax.rem(chan + groups - p, groups)
         leaving += spread_block(out_ref, block, p, reach, groups, place, sems[6:8])
+    finish_blocks(out_ref, leaving, reach, groups, place, sems[6:8])
     for copy in copies + list(handing.values()):
         copy.wait_send()
-    for copy in leaving:
-        copy.wait()
 
 
 def last_kernel(reach, layer, collected_ref, state_ref, mix_ref, out_ref, back, sums, heard, ready, *sems):

time: 144 us -> 144 us (level); the launches traced: 142 us -> 145 us
  Pallas kernels: 130 us -> 133 us
    pallas_call x2, Pallas kernels: 25 us -> 41.4 us  [pair_messages(): pl.pallas_call(functools.partial(pair_kernel, blocks), out_shape=jax.Shap...]
    pallas_call x3, Pallas kernels: 104 us -> 91.5 us  [remote_call(): pl.pallas_call(kernel, out_shape=[jax.ShapeDtypeStruct(shape, jnp.float32...]
where the time goes in v7:
time: 144 us; the launch traced here: 145 us
  Pallas kernels  133 us (92%)
  local copies, waits for them, and re-layouts  10.5 us (7%)
  other arithmetic  1.57 us (1%)
    pallas_call x3, Pallas kernels, remote_call(): pl.pallas_call(kernel, out_shape=[jax.ShapeDtypeStruct(shape, jnp.float32...  91.5 us
    pallas_call x2, Pallas kernels, pair_messages(): pl.pallas_call(functools.partial(pair_kernel, blocks), out_shape=jax.Shap...  41.4 us
    unnamed x25, local copies, waits for them, and re-layouts  9.76 us

profile of v7, /device:TPU:0, one launch (start us, length us, event | category | flops | bytes accessed | tf_op | source)
XLA Modules:
  0.0 145.1 jit_solution(2988402135503942082)
XLA Ops:
  0.0 0.7 compare_convert_fusion
  0.7 0.1 pad.2.clone
  0.8 0.8 maximum_bitcast_fusion.geometry_ref
  1.6 0.0 copy-start.6
  1.6 1.0 copy-done.6
  2.6 0.0 copy-start.7
  2.6 1.0 copy-done.7
  3.7 0.0 copy-start.8
  3.7 0.9 copy-done.8
  4.6 42.8 %shard_map.73 = (f32[12,128,128]{2,1,0:T(8,128)S(1)}, f32[4,128,128]{2,1,0:T(8,128)S(1)}, f32[12,8,128]{2,1,0:T(8,128)S(1)}, f32[12,128,8]{2,1,0:T(8,128)S(1)}, ...) custom-call(f32[4,8,128]{2,1,0:T(8,128)S(1)} %maximum_bitcast_fusion.geometry_ref, ...), custom_call_target="tpu_custom_call" | custom-call | tf_op jit(solution)/shard_map/pallas_call | solution.py:540
  47.4 0.0 copy-start
  47.4 1.0 copy-done
  48.4 0.0 copy-start.2
  48.4 0.9 copy-done.2
  49.3 0.7 fusion
  50.0 0.1 copy.12
  50.1 0.1 pad_add_fusion.base_ref
  50.2 1.2 copy-done.3
  51.4 0.7 copy-done.9
  52.1 20.7 %shard_map.74.collected_ref = f32[12,128,128]{2,1,0:T(8,128)S(1)} custom-call(s32[2]{0:T(128)S(1)} %pad_add_fusion.base_ref, s32[3,64]{1,0:T(4,128)S(1)} %copy-done.9, f32[12,128,8]{2,1,0:T(8,128)S(1)} %get-tuple-element.13.columns_ref, f32[12,8,128]{2,1,0:T(8,128)S(1)} %get-tuple-element.14.rows_ref, f32[12,128,128]{2,1,0:T(8,128)S(1)} %copy-done.3, ...), custom_call_target="tpu_custom_call" | custom-call | tf_op jit(solution)/shard_map/pallas_call | solution.py:191
  72.9 0.0 copy-done.1
  72.9 0.0 copy-start.10
  72.9 26.7 %shard_map.75 = (f32[12,128,128]{2,1,0:T(8,128)S(1)}, f32[4,128,128]{2,1,0:T(8,128)S(1)}) custom-call(f32[12,128,128]{2,1,0:T(8,128)S(1)} %shard_map.74.collected_ref, f32[4,128,128]{2,1,0:T(8,128)S(1)} %get-tuple-element.16.state_ref, f32[8,4,2,64,128]{4,3,2,1,0:T(8,128)S(1)} %get-tuple-element.17.mix_ref, f32[8,4,1,16,512]{4,3,2,1,0:T(8,128)S(1)} %copy-done.1), custom_call_target="tpu_custom_call" | custom-call | tf_op jit(solution)/shard_map/pallas_call | solution.py:540
  99.6 0.0 copy-start.4
  99.6 0.9 copy-done.4
  100.5 0.1 copy.13
  100.6 0.0 copy-done.10
  100.6 0.0 copy-start.5
  100.6 1.1 copy-done.5
  101.7 20.7 %shard_map.76.collected_ref = f32[12,128,128]{2,1,0:T(8,128)S(1)} custom-call(s32[2]{0:T(128)S(1)} %pad_add_fusion.base_ref, s32[3,64]{1,0:T(4,128)S(1)} %copy-done.10, f32[12,128,8]{2,1,0:T(8,128)S(1)} %get-tuple-element.13.columns_ref, f32[12,8,128]{2,1,0:T(8,128)S(1)} %get-tuple-element.14.rows_ref, f32[12,128,128]{2,1,0:T(8,128)S(1)} %copy-done.5, ...), custom_call_target="tpu_custom_call" | custom-call | tf_op jit(solution)/shard_map/pallas_call | solution.py:191
  122.4 22.0 %shard_map.77 = f32[128,512]{1,0:T(8,128)S(1)} custom-call(f32[12,128,128]{2,1,0:T(8,128)S(1)} %shard_map.76.collected_ref, f32[4,128,128]{2,1,0:T(8,128)S(1)} %get-tuple-element.20.state_ref, f32[8,4,2,64,128]{4,3,2,1,0:T(8,128)S(1)} %get-tuple-element.17.mix_ref), custom_call_target="tpu_custom_call" | custom-call | tf_op jit(solution)/shard_map/pallas_call | solution.py:540
  144.4 0.7 copy.17
  (4 shorter events, 0.0 us)
Async XLA Ops:
  1.6 1.0 copy-start.6
  2.6 1.0 copy-start.7
  3.7 0.9 copy-start.8
  47.4 1.0 copy-start
  48.4 0.9 copy-start.2
  50.1 22.7 %copy-start.1 = (f32[8,4,1,16,512]{4,3,2,1,0:T(8,128)S(1)}, f32[8,4,1,16,512]{4,3,2,1,0:T(8,128)}, u32[]{:S(2)}) copy-start(f32[8,4,1,16,512]{4,3,2,1,0:T(8,128)} %copy-done) | copy-start | bytes 3145732
  50.2 1.2 copy-start.3
  51.4 0.7 copy-start.9
  72.9 27.7 %copy-start.10 = (s32[3,64]{1,0:T(4,128)S(1)}, s32[3,64]{1,0:T(4,128)}, u32[]{:S(2)}) copy-start(s32[3,64]{1,0:T(4,128)} %table_ref.3) | copy-start | bytes 2308
  99.6 0.9 copy-start.4
  100.6 1.1 copy-start.5

commit v8 on v7

--- a/solution.py
+++ b/solution.py
@@ -534,7 +534,7 @@
         copy.wait_send()
 
 
-def remote_call(kernel, outs, scratch, pairs, collective, *operands, elsewhere=0):
+def remote_call(kernel, outs, scratch, pairs, collective, *operands, elsewhere=0, grant=40):
     vmem = pl.BlockSpec(memory_space=pltpu.VMEM)
     sems = [pltpu.SemaphoreType.DMA(shape) for shape in pairs for _ in range(2)]
     return pl.pallas_call(
@@ -545,7 +545,7 @@
         out_specs=[vmem] * len(outs),
         scratch_shapes=[pltpu.VMEM(shape, jnp.float32) for shape in scratch] + sems,
         compiler_params=pltpu.CompilerParams(
-            collective_id=collective, has_side_effects=True, vmem_limit_bytes=40 * 1024 * 1024
+            collective_id=collective, has_side_effects=True, vmem_limit_bytes=grant * 1024 * 1024
         ),
     )(*operands)
 
@@ -587,6 +587,7 @@
         in_weight,
         mix_weight,
         elsewhere=3,
+        grant=60,
     )
     scratch = [(reach, groups, *square), (groups, *square), (groups - 1, *square)]
     for layer in range(LAYERS - 1):

time: 144 us -> 145 us (level); the launches traced: 145 us -> 143 us
  local copies, waits for them, and re-layouts: 10.5 us -> 8.86 us
    pallas_call x2, Pallas kernels: 41.4 us -> 30.5 us  [pair_messages(): pl.pallas_call(functools.partial(pair_kernel, blocks), out_shape=jax.Shap...]
    pallas_call x3, Pallas kernels: 91.5 us -> 102 us  [remote_call(): pl.pallas_call(kernel, out_shape=[jax.ShapeDtypeStruct(shape, jnp.float32...]
    unnamed x25 -> x27, local copies, waits for them, and re-layouts: 9.76 us -> 7.92 us
where the time goes in v8:
time: 145 us; the launch traced here: 143 us
  Pallas kernels  132 us (91%)
  local copies, waits for them, and re-layouts  8.86 us (6%)
  other arithmetic  2.17 us (1%)
    pallas_call x3, Pallas kernels, remote_call(): pl.pallas_call(kernel, out_shape=[jax.ShapeDtypeStruct(shape, jnp.float32...  102 us
    pallas_call x2, Pallas kernels, pair_messages(): pl.pallas_call(functools.partial(pair_kernel, blocks), out_shape=jax.Shap...  30.5 us
    unnamed x27, local copies, waits for them, and re-layouts  7.92 us

profile of v8, /device:TPU:0, one launch (start us, length us, event | category | flops | bytes accessed | tf_op | source)
XLA Modules:
  0.0 143.3 jit_solution(4886459441747857274)
XLA Ops:
  0.0 0.7 compare_convert_fusion
  0.7 0.1 pad.2.clone
  0.8 1.4 maximum_bitcast_fusion.geometry_ref
  2.2 45.9 %shard_map.73 = (f32[12,128,128]{2,1,0:T(8,128)}, f32[4,128,128]{2,1,0:T(8,128)}, f32[12,8,128]{2,1,0:T(8,128)}, f32[12,128,8]{2,1,0:T(8,128)}, f32[8,4,2,64,128...) custom-call(f32[4,8,128]{2,1,0:T(8,128)} %maximum_bitcast_fusion.geometry_ref, f32[128,512]{1,0:T(8,128)} %feature_ref.1, ...), custom_call_target="tpu_custom_call" | custom-call | tf_op jit(solution)/shard_map/pallas_call | solution.py:540
  48.1 0.0 copy-start
  48.1 0.9 fusion
  49.0 0.1 copy.12
  49.1 0.1 pad_add_fusion.base_ref
  49.1 0.0 copy-start.1
  49.1 1.1 copy-done.1
  50.3 0.0 copy-start.4
  50.3 1.1 copy-done.4
  51.4 0.0 copy-start.8
  51.4 0.8 copy-done.8
  52.2 0.7 copy-done.10
  52.9 15.3 %shard_map.74.collected_ref = f32[12,128,128]{2,1,0:T(8,128)S(1)} custom-call(s32[2]{0:T(128)S(1)} %pad_add_fusion.base_ref, s32[3,64]{1,0:T(4,128)S(1)} %copy-done.10, f32[12,128,8]{2,1,0:T(8,128)S(1)} %copy-done.1, f32[12,8,128]{2,1,0:T(8,128)S(1)} %copy-done.8, f32[12,128,128]{2,1,0:T(8,128)S(1)} %copy-done.4, f32[8,128]{1,0:T(8,128)S(1)} %get-tuple-element.22.filter_ref, ...), custom_call_target="tpu_custom_call" | custom-call | tf_op jit(solution)/shard_map/pallas_call | solution.py:191
  68.1 0.0 copy-done
  68.2 0.0 copy-done.7
  68.2 0.0 copy-start.3
  68.2 1.2 copy-done.3
  69.4 30.9 %shard_map.75 = (f32[12,128,128]{2,1,0:T(8,128)S(1)}, f32[4,128,128]{2,1,0:T(8,128)S(1)}) custom-call(f32[12,128,128]{2,1,0:T(8,128)S(1)} %shard_map.74.collected_ref, f32[4,128,128]{2,1,0:T(8,128)S(1)} %copy-done.7, f32[8,4,2,64,128]{4,3,2,1,0:T(8,128)S(1)} %copy-done, f32[8,4,1,16,512]{4,3,2,1,0:T(8,128)S(1)} %copy-done.3), custom_call_target="tpu_custom_call" | custom-call | tf_op jit(solution)/shard_map/pallas_call | solution.py:540
  100.3 0.0 copy-start.5
  100.3 0.9 copy-done.5
  101.2 0.1 copy.13
  101.3 0.0 copy-done.2
  101.3 0.0 copy-done.9
  101.3 0.0 copy-done.11
  101.3 0.0 copy-start.6
  101.3 1.1 copy-done.6
  102.4 15.2 %shard_map.76.collected_ref = f32[12,128,128]{2,1,0:T(8,128)S(1)} custom-call(s32[2]{0:T(128)S(1)} %pad_add_fusion.base_ref, s32[3,64]{1,0:T(4,128)S(1)} %copy-done.11, f32[12,128,8]{2,1,0:T(8,128)S(1)} %copy-done.2, f32[12,8,128]{2,1,0:T(8,128)S(1)} %copy-done.9, f32[12,128,128]{2,1,0:T(8,128)S(1)} %copy-done.6, f32[8,128]{1,0:T(8,128)S(1)} %get-tuple-element.23.filter_ref, ...), custom_call_target="tpu_custom_call" | custom-call | tf_op jit(solution)/shard_map/pallas_call | solution.py:191
  117.7 25.0 %shard_map.77 = f32[128,512]{1,0:T(8,128)S(1)} custom-call(f32[12,128,128]{2,1,0:T(8,128)S(1)} %shard_map.76.collected_ref, f32[4,128,128]{2,1,0:T(8,128)S(1)} %get-tuple-element.20.state_ref, f32[8,4,2,64,128]{4,3,2,1,0:T(8,128)S(1)} %copy-done), custom_call_target="tpu_custom_call" | custom-call | tf_op jit(solution)/shard_map/pallas_call | solution.py:540
  142.6 0.7 copy.17
  (6 shorter events, 0.0 us)
Async XLA Ops:
  48.1 20.1 %copy-start = (f32[8,4,2,64,128]{4,3,2,1,0:T(8,128)S(1)}, f32[8,4,2,64,128]{4,3,2,1,0:T(8,128)}, u32[]{:S(2)}) copy-start(f32[8,4,2,64,128]{4,3,2,1,0:T(8,128)} %get-tuple-element.17.mix_ref) | copy-start | bytes 6291460
  49.1 1.1 copy-start.1
  50.3 1.1 copy-start.4
  51.4 0.8 copy-start.8
  52.2 0.7 copy-start.10
  52.9 15.3 %copy-start.7 = (f32[4,128,128]{2,1,0:T(8,128)S(1)}, f32[4,128,128]{2,1,0:T(8,128)}, u32[]{:S(2)}) copy-start(f32[4,128,128]{2,1,0:T(8,128)} %get-tuple-element.16.state_ref) | copy-start | bytes 786436
  68.2 1.2 copy-start.3
  69.4 31.9 %copy-start.2 = (f32[12,128,8]{2,1,0:T(8,128)S(1)}, f32[12,128,8]{2,1,0:T(8,128)}, u32[]{:S(2)}) copy-start(f32[12,128,8]{2,1,0:T(8,128)} %get-tuple-element.13.columns_ref) | copy-start | bytes 147460
  69.4 31.9 %copy-start.9 = (f32[12,8,128]{2,1,0:T(8,128)S(1)}, f32[12,8,128]{2,1,0:T(8,128)}, u32[]{:S(2)}) copy-start(f32[12,8,128]{2,1,0:T(8,128)} %get-tuple-element.14.rows_ref) | copy-start | bytes 147460
  69.4 31.9 %copy-start.11 = (s32[3,64]{1,0:T(4,128)S(1)}, s32[3,64]{1,0:T(4,128)}, u32[]{:S(2)}) copy-start(s32[3,64]{1,0:T(4,128)} %table_ref.3) | copy-start | bytes 2308
  100.3 0.9 copy-start.5
  101.3 1.1 copy-start.6
